TPU v7x, 256 devices: a whole 4x4x8 slice. The times are simulated.
256 devices in a mesh: ctx: 32 (over z_hi, y, core), tp: 8 (over x, z_lo).
Axes of the slice: x: 4, y: 4, z: 8 (z_hi: 4, z_lo: 2; z = z_hi * 2 + z_lo), core: 2. Of those that a mesh axis runs over, the one named last changes fastest.
Arguments:
- query_proj: bfloat16 [8192, 8192], P('ctx', 'tp'), may hold values from -6 to 6
- key_proj: bfloat16 [8192, 8192], P('ctx', 'tp'), may hold values from -6 to 6
- value_proj: bfloat16 [8192, 8192], P('ctx', 'tp'), may hold values from -6 to 6
- cotangent: bfloat16 [8192, 8192], P('ctx', 'tp'), may hold values from -6 to 6
- filter_taps: bfloat16 [8192, 8192], P(('ctx', 'tp')), may hold values from -94.552125 to 94.552125
Outputs:
- block_output: bfloat16 [8192, 8192], P('ctx', 'tp')
- grad_query: bfloat16 [8192, 8192], P('ctx', 'tp')
- grad_key: bfloat16 [8192, 8192], P('ctx', 'tp')
- grad_value: bfloat16 [8192, 8192], P('ctx', 'tp')
- grad_filter: bfloat16 [8192, 8192], P(('ctx', 'tp'))
All inputs are finite; a program needn't handle non-finite values.
Results may differ from a plain program's by a relative error of at most 0.0058.
Values may be sent and summed in bfloat16 or wider, within the bound.
No kernel may reach another device: no remote copies, remote signals or barrier semaphores. Data moves between devices by JAX's collectives and lax.ppermute only.
A program may use at most 128 MiB of HBM per device.

v0:
```python
import functools
import math

import jax
import jax.numpy as jnp
import ml_dtypes
import numpy as np
from jax import lax
from jax.experimental import pallas as pl
from jax.experimental.pallas import tpu as pltpu
from jax.sharding import PartitionSpec as P

F32 = jnp.float32
BF16 = jnp.bfloat16
LANES = 128
KEPT = 72
MIB = 1 << 20


def split_table(table):
    high = table.astype(ml_dtypes.bfloat16)
    low = (table - high.astype(np.float64)).astype(ml_dtypes.bfloat16)
    return high, low


def make_tables(seq_len):
    radix = 2 * seq_len // LANES
    blocks = radix // 2
    total = 2 * seq_len
    kept = radix // 2 + 1
    order = np.concatenate([np.arange(0, blocks, 2), np.arange(1, blocks, 2)])
    k1 = np.arange(KEPT)
    live = (k1 < kept).astype(np.float64)
    turn = 2 * math.pi * np.outer(k1, order) / radix
    first = np.concatenate([np.cos(turn) * live[:, None], -np.sin(turn) * live[:, None]], 0)
    first_table = np.concatenate(split_table(first), 1)
    lane = np.arange(LANES)
    twist = 2 * math.pi * np.outer(k1, lane) / total
    twist_real = np.tile(np.cos(twist), (1, 2)).astype(np.float32)
    twist_imag = np.tile(-np.sin(twist), (1, 2)).astype(np.float32)
    inner = 2 * math.pi * np.outer(lane, lane) / LANES
    cos, sin = np.cos(inner), np.sin(inner)
    ahead = split_table(np.block([[cos, -sin], [sin, cos]]))
    ahead_table = np.concatenate([ahead[0], ahead[0], ahead[1]], 0)
    back = split_table(np.block([[cos, sin], [-sin, cos]]))
    back_table = np.concatenate([back[0], back[0], back[1]], 0)
    weight = np.where((k1 == 0) | (k1 == radix // 2), 1.0, 2.0) * live
    weight = weight * seq_len ** (-0.5) / total
    last = split_table(np.concatenate([np.cos(turn.T) * weight, -np.sin(turn.T) * weight], 1))
    last_table = np.concatenate([last[0], last[0], last[1]], 1)
    return first_table, twist_real, twist_imag, ahead_table, back_table, last_table


def split_value(value):
    high = value.astype(BF16)
    low = (value - high.astype(F32)).astype(BF16)
    return high, low


def gather_kernel(query, key, value, cotangent, taps, out):
    width = query.shape[1]
    groups, rows, positions = out.shape
    lanes = rows // 3

    def place(start, array):
        turned = array.T.astype(BF16)
        out[:, start : start + lanes, :] = turned.reshape(groups, lanes, positions)

    place(0, key[...].astype(F32) * value[...].astype(F32))
    place(lanes, cotangent[...].astype(F32) * query[...].astype(F32))
    place(2 * lanes, taps[...].astype(F32))


def scatter_kernel(
    query, key, value, cotangent, back, block_output, grad_query, grad_key, grad_value, grad_filter
):
    groups, rows, positions = back.shape
    lanes = rows // 3

    def take(start):
        wide = back[:, start : start + lanes, :].astype(F32)
        return wide.reshape(groups * lanes, positions).T

    convolved = take(0)
    block_output[...] = (query[...].astype(F32) * convolved).astype(BF16)
    grad_query[...] = (cotangent[...].astype(F32) * convolved).astype(BF16)
    adjoint = take(lanes)
    grad_key[...] = (adjoint * value[...].astype(F32)).astype(BF16)
    grad_value[...] = (adjoint * key[...].astype(F32)).astype(BF16)
    grad_filter[...] = take(2 * lanes).astype(BF16)


def long_kernel(
    received, first, twist_real, twist_imag, ahead, back, last, out, even, odd, stage, spec_x, spec_g, spec_h
):
    sources, rows, positions = received.shape
    lanes = rows // 3
    chunk = 4

    def spectrum(start, spec):
        whole = received[:, start : start + lanes, :].astype(F32).reshape(sources * lanes, positions)
        even[...] = whole[:, :LANES]
        odd[...] = whole[:, LANES:]

        @pl.loop(0, lanes // 2)
        def _(pair):
            one = pl.ds(2 * pair, sources, stride=lanes)
            two = pl.ds(2 * pair + 1, sources, stride=lanes)
            both = jnp.concatenate(
                [
                    jnp.concatenate([even[one, :], even[two, :]], 1),
                    jnp.concatenate([odd[one, :], odd[two, :]], 1),
                ],
                0,
            ).astype(BF16)
            turned = jnp.dot(
                first[...], jnp.concatenate([both, both], 0), preferred_element_type=F32
            )
            real, imag = turned[:KEPT], turned[KEPT:]
            new_real = real * twist_real[...] - imag * twist_imag[...]
            new_imag = imag * twist_real[...] + real * twist_imag[...]
            at = pl.multiple_of(pair * 2 * KEPT, 2 * KEPT)
            stage[pl.ds(at, KEPT), :LANES] = new_real[:, :LANES]
            stage[pl.ds(at, KEPT), LANES:] = new_imag[:, :LANES]
            stage[pl.ds(at + KEPT, KEPT), :LANES] = new_real[:, LANES:]
            stage[pl.ds(at + KEPT, KEPT), LANES:] = new_imag[:, LANES:]

        @pl.loop(0, lanes // chunk)
        def _(step):
            at = pl.ds(pl.multiple_of(step * chunk * KEPT, chunk * KEPT), chunk * KEPT)
            high, low = split_value(stage[at, :])
            spec[at, :] = jnp.dot(
                jnp.concatenate([high, low, high], 1), ahead[...], preferred_element_type=F32
            )

    def finish(start, left, right, sign):
        @pl.loop(0, lanes // chunk)
        def _(step):
            at = pl.ds(pl.multiple_of(step * chunk * KEPT, chunk * KEPT), chunk * KEPT)
            left_real, left_imag = left[at, :LANES], left[at, LANES:]
            right_real, right_imag = right[at, :LANES], sign * right[at, LANES:]
            real = left_real * right_real - left_imag * right_imag
            imag = left_real * right_imag + left_imag * right_real
            high, low = split_value(jnp.concatenate([real, imag], 1))
            turned = jnp.dot(
                jnp.concatenate([high, low, high], 1), back[...], preferred_element_type=F32
            )
            for one in range(chunk):
                real = turned[one * KEPT : (one + 1) * KEPT, :LANES]
                imag = turned[one * KEPT : (one + 1) * KEPT, LANES:]
                cos, sin = twist_real[:, :LANES], twist_imag[:, :LANES]
                row = pl.ds(pl.multiple_of((step * chunk + one) * KEPT, KEPT), KEPT)
                stage[row, :LANES] = real * cos + imag * sin
                stage[row, LANES:] = imag * cos - real * sin

        @pl.loop(0, lanes // 2)
        def _(pair):
            at = pl.multiple_of(pair * 2 * KEPT, 2 * KEPT)
            one = stage[pl.ds(at, KEPT), :]
            two = stage[pl.ds(at + KEPT, KEPT), :]
            both = jnp.concatenate(
                [
                    jnp.concatenate([one[:, :LANES], two[:, :LANES]], 1),
                    jnp.concatenate([one[:, LANES:], two[:, LANES:]], 1),
                ],
                0,
            )
            high, low = split_value(both)
            signal = jnp.dot(
                last[...], jnp.concatenate([high, low, high], 0), preferred_element_type=F32
            )
            for which in range(2):
                row = pl.ds(2 * pair + which, sources, stride=lanes)
                half = signal[:, which * LANES : (which + 1) * LANES]
                even[row, :] = half[:sources]
                odd[row, :] = half[sources:]

        whole = jnp.concatenate([even[...], odd[...]], 1).astype(BF16)
        out[:, start : start + lanes, :] = whole.reshape(sources, lanes, positions)

    spectrum(0, spec_x)
    spectrum(lanes, spec_g)
    spectrum(2 * lanes, spec_h)
    finish(0, spec_h, spec_x, 1.0)
    finish(lanes, spec_g, spec_h, -1.0)
    finish(2 * lanes, spec_g, spec_x, -1.0)


def gather(query, key, value, cotangent, taps, ranks):
    positions, width = query.shape
    lanes = width // ranks
    groups = LANES // lanes
    column = pl.BlockSpec((positions, LANES), lambda i: (0, i))
    return pl.pallas_call(
        gather_kernel,
        grid=(width // LANES,),
        in_specs=[column] * 5,
        out_specs=pl.BlockSpec((groups, 3 * lanes, positions), lambda i: (i, 0, 0)),
        out_shape=jax.ShapeDtypeStruct((ranks, 3 * lanes, positions), BF16),
        compiler_params=pltpu.CompilerParams(vmem_limit_bytes=24 * MIB),
        cost_estimate=pl.CostEstimate(flops=10**6, bytes_accessed=4 * MIB, transcendentals=0),
    )(query, key, value, cotangent, taps)


def scatter(query, key, value, cotangent, back):
    positions, width = query.shape
    ranks, rows, _ = back.shape
    groups = LANES // (width // ranks)
    column = pl.BlockSpec((positions, LANES), lambda i: (0, i))
    return pl.pallas_call(
        scatter_kernel,
        grid=(width // LANES,),
        in_specs=[column] * 4 + [pl.BlockSpec((groups, rows, positions), lambda i: (i, 0, 0))],
        out_specs=[column] * 5,
        out_shape=[jax.ShapeDtypeStruct((positions, width), BF16)] * 5,
        compiler_params=pltpu.CompilerParams(vmem_limit_bytes=24 * MIB),
        cost_estimate=pl.CostEstimate(flops=10**6, bytes_accessed=6 * MIB, transcendentals=0),
    )(query, key, value, cotangent, back)


def long_convolution(received):
    sources, rows, positions = received.shape
    lanes = rows // 3
    tables = [jnp.asarray(table) for table in make_tables(sources * positions)]
    spectra = pltpu.VMEM((lanes * KEPT, 2 * LANES), F32)
    return pl.pallas_call(
        long_kernel,
        out_shape=jax.ShapeDtypeStruct(received.shape, BF16),
        scratch_shapes=[pltpu.VMEM((sources * lanes, LANES), F32)] * 2 + [spectra] * 4,
        compiler_params=pltpu.CompilerParams(vmem_limit_bytes=48 * MIB),
        cost_estimate=pl.CostEstimate(flops=10**10, bytes_accessed=3 * MIB, transcendentals=0),
    )(received, *tables)


def local(query_proj, key_proj, value_proj, cotangent, filter_taps):
    ranks = lax.axis_size("ctx")
    taps = lax.all_to_all(filter_taps, "tp", split_axis=1, concat_axis=0, tiled=True)
    sent = gather(query_proj, key_proj, value_proj, cotangent, taps, ranks)
    received = lax.all_to_all(sent, "ctx", split_axis=0, concat_axis=0, tiled=True)
    made = long_convolution(received)
    back = lax.all_to_all(made, "ctx", split_axis=0, concat_axis=0, tiled=True)
    outputs = scatter(query_proj, key_proj, value_proj, cotangent, back)
    grad_filter = lax.all_to_all(outputs[4], "tp", split_axis=0, concat_axis=1, tiled=True)
    return (*outputs[:4], grad_filter)


def solution(mesh):
    placed = (P("ctx", "tp"),) * 4 + (P(("ctx", "tp"), None),)
    return jax.shard_map(local, mesh=mesh, in_specs=placed, out_specs=placed, check_vma=False)
```

profile of v0, /device:TPU:34, one launch (start us, length us, event | category | flops | bytes accessed | tf_op | source)
XLA Modules:
  0.0 165.2 jit_solution(15292603752900560819)
XLA Ops:
  0.6 0.0 copy-start.3
  0.6 0.0 copy-start.2
  0.7 0.0 copy-start.1
  0.7 0.0 copy-start
  0.7 1.2 copy.21
  1.9 13.5 %all_to_all.48 = bf16[32,8,1024]{2,0,1:T(8,128)(2,1)S(1)} all-to-all(bf16[32,8,1024]{2,0,1:T(8,128)(2,1)S(1)} %bitcast.14), channel_id=1, replica_groups=mesh['ctx'=32,'tp'=8] {'tp'}, dimensions={1} | all-to-all | bytes 1048576 | tf_op jit(solution)/shard_map/all_to_all | solution.py:237
  15.4 0.0 copy-done.3
  15.4 0.0 copy-done.2
  15.4 0.0 copy-done.1
  15.5 0.0 copy-done
  15.5 2.0 %shard_map.146 = bf16[32,96,256]{2,1,0:T(8,128)(2,1)S(1)} custom-call(bf16[256,1024]{1,0:T(8,128)(2,1)S(1)} %copy-done, bf16[256,1024]{1,0:T(8,128)(2,1)S(1)} %copy-done.1, bf16[256,1024]{1,0:T(8,128)(2,1)S(1)} %copy-done.2, bf16[256,1024]{1,0:T(8,128)(2,1)S(1)} %copy-done.3, bf16[256,1024]{1,0:T(8,128)(2,1)S(1)} %bitcast.11), custom_call_target="tpu_custom_call" | custom-call | flops 1000000 | bytes 4194304 | tf_op jit(solution)/shard_map/pallas_call | solution.py:194
  17.4 0.0 copy-start.4
  17.4 0.0 copy-start.5
  17.4 0.0 copy-start.6
  17.5 0.0 copy-start.7
  17.5 0.0 copy-start.8
  17.5 0.0 copy-start.9
  17.5 51.5 %all_to_all.49.received = bf16[32,96,256]{2,1,0:T(8,128)(2,1)S(1)} all-to-all(bf16[32,96,256]{2,1,0:T(8,128)(2,1)S(1)} %shard_map.146), channel_id=1, replica_groups=mesh['ctx'=32,'tp'=8] {'ctx'}, dimensions={0} | all-to-all | bytes 3145728 | tf_op jit(solution)/shard_map/all_to_all | solution.py:239
  69.0 0.0 copy-done.4
  69.0 0.0 copy-done.5
  69.0 0.0 copy-done.6
  69.0 0.0 copy-done.7
  69.0 0.0 copy-done.8
  69.0 0.0 copy-done.9
  69.0 33.3 %shard_map.147 = bf16[32,96,256]{2,1,0:T(8,128)(2,1)S(1)} custom-call(bf16[32,96,256]{2,1,0:T(8,128)(2,1)S(1)} %all_to_all.49.received, bf16[144,128]{1,0:T(8,128)(2,1)S(1)} %copy-done.9, f32[72,256]{1,0:T(8,128)S(1)} %copy-done.7, f32[72,256]{1,0:T(8,128)S(1)} %copy-done.6, bf16[768,256]{1,0:T(8,128)(2,1)S(1)} %copy-done.5, bf16[768,256]{1,0:T(8,128)(2,1)S(1)} %copy-done.4, ...), custom_call_target="tpu_custom_call" | custom-call | flops 10000000000 | bytes 3145728 | tf_op jit(solution)/shard_map/pallas_call | solution.py:226
  102.3 45.2 %all_to_all.50.back = bf16[32,96,256]{2,1,0:T(8,128)(2,1)S(1)} all-to-all(bf16[32,96,256]{2,1,0:T(8,128)(2,1)S(1)} %shard_map.147), channel_id=1, replica_groups=mesh['ctx'=32,'tp'=8] {'ctx'}, dimensions={0} | all-to-all | bytes 3145728 | tf_op jit(solution)/shard_map/all_to_all | solution.py:241
  147.5 3.8 %shard_map.148 = (bf16[256,1024]{1,0:T(8,128)(2,1)}, bf16[256,1024]{1,0:T(8,128)(2,1)}, bf16[256,1024]{1,0:T(8,128)(2,1)}, bf16[256,1024]{1,0:T(8,128)(2,1)}, bf16[256,1024]{1,0:T(8,128)(2,1)S(1)}) custom-call(bf16[256,1024]{1,0:T(8,128)(2,1)S(1)} %copy-done, bf16[256,1024]{1,0:T(8,128)(2,1)S(1)} %copy-done.1, bf16[256,1024]{1,0:T(8,128)(2,1)S(1)} %copy-done.2, ...), custom_call_target="tpu_custom_call" | custom-call | flops 1000000 | bytes 6291456 | tf_op jit(solution)/shard_map/pallas_call | solution.py:210
  151.4 13.0 %all_to_all.51 = bf16[8,32,1024]{2,1,0:T(8,128)(2,1)S(1)} all-to-all(bf16[8,32,1024]{2,1,0:T(8,128)(2,1)S(1)} %bitcast.12), channel_id=1, replica_groups=mesh['ctx'=32,'tp'=8] {'tp'}, dimensions={0} | all-to-all | bytes 1048576 | tf_op jit(solution)/shard_map/all_to_all | solution.py:243
  164.3 0.8 copy.19
Async XLA Ops:
  0.6 14.8 %copy-start.3 = (bf16[256,1024]{1,0:T(8,128)(2,1)S(1)}, bf16[256,1024]{1,0:T(8,128)(2,1)}, u32[]{:S(2)}) copy-start(bf16[256,1024]{1,0:T(8,128)(2,1)} %cotangent.3) | copy-start | bytes 1572868
  0.6 14.8 %copy-start.2 = (bf16[256,1024]{1,0:T(8,128)(2,1)S(1)}, bf16[256,1024]{1,0:T(8,128)(2,1)}, u32[]{:S(2)}) copy-start(bf16[256,1024]{1,0:T(8,128)(2,1)} %value.3) | copy-start | bytes 1572868
  0.7 14.8 %copy-start.1 = (bf16[256,1024]{1,0:T(8,128)(2,1)S(1)}, bf16[256,1024]{1,0:T(8,128)(2,1)}, u32[]{:S(2)}) copy-start(bf16[256,1024]{1,0:T(8,128)(2,1)} %key.3) | copy-start | bytes 1572868
  0.7 14.8 %copy-start = (bf16[256,1024]{1,0:T(8,128)(2,1)S(1)}, bf16[256,1024]{1,0:T(8,128)(2,1)}, u32[]{:S(2)}) copy-start(bf16[256,1024]{1,0:T(8,128)(2,1)} %query.3) | copy-start | bytes 1572868
  17.4 51.6 %copy-start.4 = (bf16[768,256]{1,0:T(8,128)(2,1)S(1)}, bf16[768,256]{1,0:T(8,128)(2,1)}, u32[]{:S(2)}) copy-start(bf16[768,256]{1,0:T(8,128)(2,1)} %constant.16.clone.back) | copy-start | bytes 1179652
  17.4 51.6 %copy-start.5 = (bf16[768,256]{1,0:T(8,128)(2,1)S(1)}, bf16[768,256]{1,0:T(8,128)(2,1)}, u32[]{:S(2)}) copy-start(bf16[768,256]{1,0:T(8,128)(2,1)} %constant.15.clone.ahead) | copy-start | bytes 1179652
  17.4 51.5 %copy-start.6 = (f32[72,256]{1,0:T(8,128)S(1)}, f32[72,256]{1,0:T(8,128)}, u32[]{:S(2)}) copy-start(f32[72,256]{1,0:T(8,128)} %constant.14.clone.twist_imag) | copy-start | bytes 221188
  17.5 51.5 %copy-start.7 = (f32[72,256]{1,0:T(8,128)S(1)}, f32[72,256]{1,0:T(8,128)}, u32[]{:S(2)}) copy-start(f32[72,256]{1,0:T(8,128)} %constant.13.clone.twist_real) | copy-start | bytes 221188
  17.5 51.5 %copy-start.8 = (bf16[64,432]{1,0:T(8,128)(2,1)S(1)}, bf16[64,432]{1,0:T(8,128)(2,1)}, u32[]{:S(2)}) copy-start(bf16[64,432]{1,0:T(8,128)(2,1)} %constant.17.clone.last) | copy-start | bytes 165892
  17.5 51.5 %copy-start.9 = (bf16[144,128]{1,0:T(8,128)(2,1)S(1)}, bf16[144,128]{1,0:T(8,128)(2,1)}, u32[]{:S(2)}) copy-start(bf16[144,128]{1,0:T(8,128)(2,1)} %constant.12.clone.first) | copy-start | bytes 110596
where the time goes:
time: 167 us; the launch traced here: 165 us
  blocking collectives  123 us (74%)
  Pallas kernels  39.1 us (23%)
  local copies, waits for them, and re-layouts  2.11 us (1%)
    all_to_all x1, blocking collectives, local(): lax.all_to_all(sent, 'ctx', split_axis=0, concat_axis=0, tiled=True)  51.5 us
    all_to_all x1, blocking collectives, local(): back = lax.all_to_all(made, 'ctx', split_axis=0, concat_axis=0, tiled=True)  45.2 us
    pallas_call x1, Pallas kernels, long_convolution(): pl.pallas_call(long_kernel, out_shape=jax.ShapeDtypeStruct(received.shape...  33.3 us
    all_to_all x1, blocking collectives, local(): lax.all_to_all(filter_taps, 'tp', split_axis=1, concat_axis=0, tiled=True)  13.5 us
    all_to_all x1, blocking collectives, local(): lax.all_to_all(outputs[4], 'tp', split_axis=0, concat_axis=1, tiled=True)  13 us
    pallas_call x1, Pallas kernels, scatter(): pl.pallas_call(scatter_kernel, grid=(width // LANES,), in_specs=[column]...  3.84 us

commit v1 on v0

v1 whole, which is shorter than its diff:
```python
import functools
import math

import jax
import jax.numpy as jnp
import ml_dtypes
import numpy as np
from jax import lax
from jax.experimental import pallas as pl
from jax.experimental.pallas import tpu as pltpu
from jax.sharding import PartitionSpec as P

F32 = jnp.float32
BF16 = jnp.bfloat16
LANES = 128
KEPT = 72
MIB = 1 << 20
CHUNK = 4


def split_table(table):
    high = table.astype(ml_dtypes.bfloat16)
    low = (table - high.astype(np.float64)).astype(ml_dtypes.bfloat16)
    return high, low


def make_tables(seq_len):
    radix = 2 * seq_len // LANES
    blocks = radix // 2
    total = 2 * seq_len
    kept = radix // 2 + 1
    order = np.concatenate([np.arange(0, blocks, 2), np.arange(1, blocks, 2)])
    k1 = np.arange(KEPT)
    live = (k1 < kept).astype(np.float64)
    turn = 2 * math.pi * np.outer(k1, order) / radix
    first = np.concatenate([np.cos(turn) * live[:, None], -np.sin(turn) * live[:, None]], 0)
    first_table = np.concatenate(split_table(first), 1)
    lane = np.arange(LANES)
    twist = 2 * math.pi * np.outer(k1, lane) / total
    twist_real = np.tile(np.cos(twist), (1, 2)).astype(np.float32)
    twist_imag = np.tile(-np.sin(twist), (1, 2)).astype(np.float32)
    inner = 2 * math.pi * np.outer(lane, lane) / LANES
    cos, sin = np.cos(inner), np.sin(inner)
    ahead = split_table(np.block([[cos, -sin], [sin, cos]]))
    ahead_table = np.concatenate([ahead[0], ahead[0], ahead[1]], 0)
    back = split_table(np.block([[cos, sin], [-sin, cos]]))
    back_table = np.concatenate([back[0], back[0], back[1]], 0)
    weight = np.where((k1 == 0) | (k1 == radix // 2), 1.0, 2.0) * live
    weight = weight * seq_len ** (-0.5) / total
    last = split_table(np.concatenate([np.cos(turn.T) * weight, -np.sin(turn.T) * weight], 1))
    last_table = np.concatenate([last[0], last[0], last[1]], 1)
    return first_table, twist_real, twist_imag, ahead_table, back_table, last_table


def split_value(value):
    high = value.astype(BF16)
    low = (value - high.astype(F32)).astype(BF16)
    return high, low


def swap_blocks(parts):
    block = lax.broadcasted_iota(jnp.int32, parts[0].shape, 1) // (LANES // 4)

    def exchange(parts, bit):
        upper = (block & bit) != 0
        shift = bit * (LANES // 4)
        new = list(parts)
        for low in range(4):
            if low & bit:
                continue
            high = low | bit
            new[low] = jnp.where(upper, pltpu.roll(parts[high], shift, 1), parts[low])
            new[high] = jnp.where(upper, parts[high], pltpu.roll(parts[low], LANES - shift, 1))
        return new

    return exchange(exchange(parts, 2), 1)


def gather_kernel(query, key, value, cotangent, taps, out):
    groups, rows, positions = out.shape
    lanes = rows // 3
    tap_rows, channels = taps.shape
    step = pl.program_id(0)

    def place(start, array):
        turned = array.T.astype(BF16)
        out[:, start : start + lanes, :] = turned.reshape(groups, lanes, positions)

    place(0, key[...].astype(F32) * value[...].astype(F32))
    place(lanes, cotangent[...].astype(F32) * query[...].astype(F32))
    for half in range(2):
        pieces = [
            taps[:, pl.ds(pl.multiple_of(tp * (channels // 8) + step * LANES, LANES), LANES)]
            for tp in range(4 * half, 4 * half + 4)
        ]
        turned = jnp.concatenate(pieces, 0).astype(F32).T.reshape(groups, 4, 8, LANES)
        swapped = swap_blocks([turned[:, one].reshape(groups * 8, LANES) for one in range(4)])
        column = slice(half * LANES, (half + 1) * LANES)
        whole = jnp.stack([part.reshape(groups, 8, LANES) for part in swapped], 1)
        out[:, 2 * lanes :, column] = whole.reshape(groups, lanes, LANES).astype(BF16)


def scatter_kernel(
    query, key, value, cotangent, back, block_output, grad_query, grad_key, grad_value, grad_filter
):
    groups, rows, positions = back.shape
    lanes = rows // 3
    tap_rows, channels = grad_filter.shape
    step = pl.program_id(0)

    def take(start):
        wide = back[:, start : start + lanes, :].astype(F32)
        return wide.reshape(groups * lanes, positions).T

    convolved = take(0)
    block_output[...] = (query[...].astype(F32) * convolved).astype(BF16)
    grad_query[...] = (cotangent[...].astype(F32) * convolved).astype(BF16)
    adjoint = take(lanes)
    grad_key[...] = (adjoint * value[...].astype(F32)).astype(BF16)
    grad_value[...] = (adjoint * key[...].astype(F32)).astype(BF16)
    for half in range(2):
        column = slice(half * LANES, (half + 1) * LANES)
        wide = back[:, 2 * lanes :, column].astype(F32).reshape(groups, 4, 8, LANES)
        swapped = swap_blocks([wide[:, one].reshape(groups * 8, LANES) for one in range(4)])
        whole = jnp.stack([part.reshape(groups, 8, LANES) for part in swapped], 1)
        turned = whole.reshape(groups * lanes, LANES).T.astype(BF16)
        for one in range(4):
            start = (4 * half + one) * (channels // 8) + step * LANES
            grad_filter[:, pl.ds(pl.multiple_of(start, LANES), LANES)] = turned[
                one * tap_rows : (one + 1) * tap_rows
            ]


def forward(channel, lanes, first, twist_real, twist_imag, ahead, stage, spec):
    @pl.loop(0, lanes // 2, unroll=True)
    def _(pair):
        even_one, odd_one = channel(2 * pair)
        even_two, odd_two = channel(2 * pair + 1)
        both = jnp.concatenate(
            [
                jnp.concatenate([even_one, even_two], 1),
                jnp.concatenate([odd_one, odd_two], 1),
            ],
            0,
        ).astype(BF16)
        turned = jnp.dot(
            first[...], jnp.concatenate([both, both], 0), preferred_element_type=F32
        )
        real, imag = turned[:KEPT], turned[KEPT:]
        new_real = real * twist_real[...] - imag * twist_imag[...]
        new_imag = imag * twist_real[...] + real * twist_imag[...]
        at = pl.multiple_of(pair * 2 * KEPT, 2 * KEPT)
        stage[pl.ds(at, KEPT), :LANES] = new_real[:, :LANES]
        stage[pl.ds(at, KEPT), LANES:] = new_imag[:, :LANES]
        stage[pl.ds(at + KEPT, KEPT), :LANES] = new_real[:, LANES:]
        stage[pl.ds(at + KEPT, KEPT), LANES:] = new_imag[:, LANES:]

    @pl.loop(0, lanes // CHUNK, unroll=True)
    def _(step):
        at = pl.ds(pl.multiple_of(step * CHUNK * KEPT, CHUNK * KEPT), CHUNK * KEPT)
        high, low = split_value(stage[at, :])
        spec[at, :] = jnp.dot(
            jnp.concatenate([high, low, high], 1), ahead[...], preferred_element_type=F32
        )


def backward(left, right, sign, put, lanes, twist_real, twist_imag, back, last, stage):
    @pl.loop(0, lanes // CHUNK, unroll=True)
    def _(step):
        at = pl.ds(pl.multiple_of(step * CHUNK * KEPT, CHUNK * KEPT), CHUNK * KEPT)
        left_real, left_imag = left[at, :LANES], left[at, LANES:]
        right_real, right_imag = right[at, :LANES], sign * right[at, LANES:]
        real = left_real * right_real - left_imag * right_imag
        imag = left_real * right_imag + left_imag * right_real
        high, low = split_value(jnp.concatenate([real, imag], 1))
        turned = jnp.dot(
            jnp.concatenate([high, low, high], 1), back[...], preferred_element_type=F32
        )
        for one in range(CHUNK):
            real = turned[one * KEPT : (one + 1) * KEPT, :LANES]
            imag = turned[one * KEPT : (one + 1) * KEPT, LANES:]
            cos, sin = twist_real[:, :LANES], twist_imag[:, :LANES]
            row = pl.ds(pl.multiple_of((step * CHUNK + one) * KEPT, KEPT), KEPT)
            stage[row, :LANES] = real * cos + imag * sin
            stage[row, LANES:] = imag * cos - real * sin

    @pl.loop(0, lanes // 2, unroll=True)
    def _(pair):
        at = pl.multiple_of(pair * 2 * KEPT, 2 * KEPT)
        one = stage[pl.ds(at, KEPT), :]
        two = stage[pl.ds(at + KEPT, KEPT), :]
        both = jnp.concatenate(
            [
                jnp.concatenate([one[:, :LANES], two[:, :LANES]], 1),
                jnp.concatenate([one[:, LANES:], two[:, LANES:]], 1),
            ],
            0,
        )
        high, low = split_value(both)
        signal = jnp.dot(
            last[...], jnp.concatenate([high, low, high], 0), preferred_element_type=F32
        )
        blocks = signal.shape[0] // 2
        for which in range(2):
            half = signal[:, which * LANES : (which + 1) * LANES]
            put(2 * pair + which, half[:blocks], half[blocks:])


def first_kernel(
    received, first, twist_real, twist_imag, ahead, back, last, grad_filter, spec_x, spec_g, even, odd, stage
):
    sources, rows, positions = received.shape
    lanes = rows // 2

    def spectrum(start, spec):
        whole = received[:, start : start + lanes, :].astype(F32).reshape(sources * lanes, positions)
        even[...] = whole[:, :LANES]
        odd[...] = whole[:, LANES:]

        def channel(index):
            row = pl.ds(index, sources, stride=lanes)
            return even[row, :], odd[row, :]

        forward(channel, lanes, first, twist_real, twist_imag, ahead, stage, spec)

    def put(index, even_part, odd_part):
        row = pl.ds(index // 8 * (sources * 8) + index % 8, sources, stride=8)
        even[row, :] = even_part
        odd[row, :] = odd_part

    spectrum(0, spec_x)
    spectrum(lanes, spec_g)
    backward(spec_g, spec_x, -1.0, put, lanes, twist_real, twist_imag, back, last, stage)
    tall = sources * 8
    for half, holder in enumerate((even, odd)):
        swapped = swap_blocks([holder[one * tall : (one + 1) * tall, :] for one in range(4)])
        for one in range(4):
            grad_filter[4 * half + one] = swapped[one].astype(BF16)


def second_kernel(
    taps, spec_x, spec_g, first, twist_real, twist_imag, ahead, back, last, out, even, odd, stage, spec_h
):
    sources, rows, positions = out.shape
    lanes = rows // 2
    tall = sources * 8
    for half, holder in enumerate((even, odd)):
        swapped = swap_blocks([taps[4 * half + one].astype(F32) for one in range(4)])
        for one in range(4):
            holder[one * tall : (one + 1) * tall, :] = swapped[one]

    def channel(index):
        row = pl.ds(index // 8 * tall + index % 8, sources, stride=8)
        return even[row, :], odd[row, :]

    def put(index, even_part, odd_part):
        row = pl.ds(index, sources, stride=lanes)
        even[row, :] = even_part
        odd[row, :] = odd_part

    def result(start, left, right, sign):
        backward(left, right, sign, put, lanes, twist_real, twist_imag, back, last, stage)
        whole = jnp.concatenate([even[...], odd[...]], 1).astype(BF16)
        out[:, start : start + lanes, :] = whole.reshape(sources, lanes, positions)

    forward(channel, lanes, first, twist_real, twist_imag, ahead, stage, spec_h)
    result(0, spec_h, spec_x, 1.0)
    result(lanes, spec_g, spec_h, -1.0)


def gather(query, key, value, cotangent, taps, ranks):
    positions, width = query.shape
    lanes = width // ranks
    groups = LANES // lanes
    column = pl.BlockSpec((positions, LANES), lambda i: (0, i))
    return pl.pallas_call(
        gather_kernel,
        grid=(width // LANES,),
        in_specs=[column] * 4 + [pl.BlockSpec(taps.shape, lambda i: (0, 0))],
        out_specs=pl.BlockSpec((groups, 3 * lanes, positions), lambda i: (i, 0, 0)),
        out_shape=jax.ShapeDtypeStruct((ranks, 3 * lanes, positions), BF16),
        compiler_params=pltpu.CompilerParams(vmem_limit_bytes=24 * MIB),
        cost_estimate=pl.CostEstimate(flops=10**6, bytes_accessed=4 * MIB, transcendentals=0),
    )(query, key, value, cotangent, taps)


def scatter(query, key, value, cotangent, back, taps_shape):
    positions, width = query.shape
    ranks, rows, _ = back.shape
    groups = LANES // (width // ranks)
    column = pl.BlockSpec((positions, LANES), lambda i: (0, i))
    return pl.pallas_call(
        scatter_kernel,
        grid=(width // LANES,),
        in_specs=[column] * 4 + [pl.BlockSpec((groups, rows, positions), lambda i: (i, 0, 0))],
        out_specs=[column] * 4 + [pl.BlockSpec(taps_shape, lambda i: (0, 0))],
        out_shape=[jax.ShapeDtypeStruct((positions, width), BF16)] * 4
        + [jax.ShapeDtypeStruct(taps_shape, BF16)],
        compiler_params=pltpu.CompilerParams(vmem_limit_bytes=24 * MIB),
        cost_estimate=pl.CostEstimate(flops=10**6, bytes_accessed=6 * MIB, transcendentals=0),
    )(query, key, value, cotangent, back)


def whole_spec(shape):
    return pl.BlockSpec(shape, lambda i: (0,) * len(shape))


def first_part(received, tables):
    sources, rows, positions = received.shape
    lanes = rows // 3
    plain = pltpu.VMEM((sources * lanes, LANES), F32)
    spectra = (lanes * KEPT, 2 * LANES)
    shapes = [(8, sources * 8, LANES), spectra, spectra]
    return pl.pallas_call(
        first_kernel,
        grid=(1,),
        in_specs=[whole_spec((sources, 2 * lanes, positions))]
        + [whole_spec(table.shape) for table in tables],
        out_specs=[whole_spec(shape) for shape in shapes],
        out_shape=[jax.ShapeDtypeStruct(shapes[0], BF16)]
        + [jax.ShapeDtypeStruct(shape, F32) for shape in shapes[1:]],
        scratch_shapes=[plain, plain, pltpu.VMEM(spectra, F32)],
        compiler_params=pltpu.CompilerParams(vmem_limit_bytes=40 * MIB),
        cost_estimate=pl.CostEstimate(flops=5 * 10**9, bytes_accessed=8 * MIB, transcendentals=0),
    )(received, *tables)


def second_part(taps, spec_x, spec_g, tables, sources, positions):
    lanes = spec_x.shape[0] // KEPT
    plain = pltpu.VMEM((sources * lanes, LANES), F32)
    operands = [taps, spec_x, spec_g, *tables]
    return pl.pallas_call(
        second_kernel,
        grid=(1,),
        in_specs=[whole_spec(operand.shape) for operand in operands],
        out_specs=whole_spec((sources, 2 * lanes, positions)),
        out_shape=jax.ShapeDtypeStruct((sources, 3 * lanes, positions), BF16),
        scratch_shapes=[plain, plain] + [pltpu.VMEM(spec_x.shape, F32)] * 2,
        compiler_params=pltpu.CompilerParams(vmem_limit_bytes=40 * MIB),
        cost_estimate=pl.CostEstimate(flops=5 * 10**9, bytes_accessed=8 * MIB, transcendentals=0),
    )(*operands)


def local(query_proj, key_proj, value_proj, cotangent, filter_taps):
    ranks = lax.axis_size("ctx")
    sent = gather(query_proj, key_proj, value_proj, cotangent, filter_taps, ranks)
    received = lax.all_to_all(sent, "ctx", split_axis=0, concat_axis=0, tiled=True)
    _, rows, positions = received.shape
    lanes = rows // 3
    tables = [jnp.asarray(table) for table in make_tables(ranks * positions)]
    taps = received[:, 2 * lanes :].reshape(ranks, 4, 8, 2, LANES).transpose(3, 1, 0, 2, 4)
    taps = lax.all_to_all(
        taps.reshape(8, ranks * 8, LANES), "tp", split_axis=0, concat_axis=0, tiled=True
    )
    grad_filter, spec_x, spec_g = first_part(received, tables)
    grad_filter = lax.all_to_all(grad_filter, "tp", split_axis=0, concat_axis=0, tiled=True)
    made = second_part(taps, spec_x, spec_g, tables, ranks, positions)
    grad_filter = grad_filter.reshape(2, 4, ranks, 8, LANES).transpose(2, 1, 3, 0, 4)
    made = made.at[:, 2 * lanes :].set(grad_filter.reshape(ranks, lanes, positions))
    back = lax.all_to_all(made, "ctx", split_axis=0, concat_axis=0, tiled=True)
    return scatter(query_proj, key_proj, value_proj, cotangent, back, filter_taps.shape)


def solution(mesh):
    placed = (P("ctx", "tp"),) * 4 + (P(("ctx", "tp"), None),)
    return jax.shard_map(local, mesh=mesh, in_specs=placed, out_specs=placed, check_vma=False)
```

time: 167 us -> 144 us (0.86)
  blocking collectives: 123 us -> 96.5 us
  Pallas kernels: 39.1 us -> 21.4 us
  starting transfers between devices: 0 us -> 11.4 us
  local copies, waits for them, and re-layouts: 2.11 us -> 13.5 us
    all_to_all x2 -> x0, blocking collectives: 26.5 us -> none  [the longest x1 13.5 us: local(): lax.all_to_all(filter_taps, 'tp', split_axis=1, concat_axis=0, tiled=True)]
    pallas_call x1 -> x2, Pallas kernels: 33.3 us -> 13.6 us  [the longest x1 7.11 us: first_part(): pl.pallas_call(first_kernel, grid=(1,), in_specs=[whole_spec((sources, 2...]
    all_to_all x0 -> x2, starting transfers between devices: none -> 11.4 us  [the longest x1 5.73 us: local(): lax.all_to_all(taps.reshape(8, ranks * 8, LANES), 'tp', split_axis=0, con...]
    unnamed x20 -> x38, local copies, waits for them, and re-layouts: 0.06 us -> 11.5 us
    all_to_all x2 -> x0, local copies, waits for them, and re-layouts: 2.05 us -> none  [the longest x1 1.22 us: local(): lax.all_to_all(filter_taps, 'tp', split_axis=1, concat_axis=0, tiled=True)]
  transfers between devices with their start and end apart: 0 -> 2, of which waited for: 0 -> 0; matrix products, arithmetic and copies ran while one was open for 0% -> 0% of each run, Pallas kernels for 0% -> 9%
where the time goes in v1:
time: 144 us
  blocking collectives  96.5 us (67%)
  Pallas kernels  21.4 us (15%)
  local copies, waits for them, and re-layouts  13.5 us (9%)
  starting transfers between devices  11.4 us (8%)
    all_to_all x1, blocking collectives, local(): lax.all_to_all(sent, 'ctx', split_axis=0, concat_axis=0, tiled=True)  50 us
    all_to_all x1, blocking collectives, local(): back = lax.all_to_all(made, 'ctx', split_axis=0, concat_axis=0, tiled=True)  46.5 us
    unnamed x38, local copies, waits for them, and re-layouts  11.5 us
    pallas_call x1, Pallas kernels, first_part(): pl.pallas_call(first_kernel, grid=(1,), in_specs=[whole_spec((sources, 2...  7.11 us
    pallas_call x1, Pallas kernels, second_part(): pl.pallas_call(second_kernel, grid=(1,), in_specs=[whole_spec(operand.sha...  6.52 us
    all_to_all x1, starting transfers between devices, local(): lax.all_to_all(taps.reshape(8, ranks * 8, LANES), 'tp', split_axis=0, con...  5.73 us
    all_to_all x1, starting transfers between devices, local(): lax.all_to_all(grad_filter, 'tp', split_axis=0, concat_axis=0, tiled=True)  5.7 us
    pallas_call x1, Pallas kernels, scatter(): pl.pallas_call(scatter_kernel, grid=(width // LANES,), in_specs=[column]...  4.68 us
  transfers between devices with their start and end apart: 2, of which 0 were waited for; matrix products, arithmetic and copies ran while one was open for 0% of the time, Pallas kernels for 9%

profile of v1, /device:TPU:34, one launch (start us, length us, event | category | flops | bytes accessed | tf_op | source)
XLA Modules:
  0.0 143.8 jit_solution(18399240119373466651)
XLA Ops:
  0.6 0.0 copy-start
  0.6 1.0 copy-done
  1.7 1.0 copy-done.2
  2.7 1.0 copy-done.4
  3.8 1.0 copy-done.6
  4.8 1.0 copy-done.8
  5.8 3.1 %shard_map.146 = bf16[32,96,256]{2,1,0:T(8,128)(2,1)S(1)} custom-call(bf16[256,1024]{1,0:T(8,128)(2,1)S(1)} %copy-done, bf16[256,1024]{1,0:T(8,128)(2,1)S(1)} %copy-done.2, bf16[256,1024]{1,0:T(8,128)(2,1)S(1)} %copy-done.4, bf16[256,1024]{1,0:T(8,128)(2,1)S(1)} %copy-done.6, bf16[32,8192]{1,0:T(8,128)(2,1)S(1)} %copy-done.8), custom_call_target="tpu_custom_call" | custom-call | flops 1000000 | bytes 4194304 | tf_op jit(solution)/shard_map/pallas_call | solution.py:276
  8.9 50.0 %all_to_all.20.received = bf16[32,96,256]{2,1,0:T(8,128)(2,1)S(1)} all-to-all(bf16[32,96,256]{2,1,0:T(8,128)(2,1)S(1)} %shard_map.146), channel_id=1, replica_groups=mesh['ctx'=32,'tp'=8] {'ctx'}, dimensions={0} | all-to-all | bytes 3145728 | tf_op jit(solution)/shard_map/all_to_all | solution.py:347
  58.9 0.0 copy-start.13
  59.0 0.0 copy-start.14
  59.0 0.9 copy.16
  59.9 5.7 %all-to-all-start.1 = ((bf16[8,256,128]{2,1,0:T(8,128)(2,1)}), bf16[8,256,128]{2,1,0:T(8,128)(2,1)S(1)}, u32[]{:S(2)}, u32[]{:S(2)}) async-start(bf16[8,256,128]{2,1,0:T(8,128)(2,1)} %bitcast.10), calls=%async_computation.1 | async-start | bytes 1048576 | tf_op jit(solution)/shard_map/all_to_all | solution.py:352
  65.6 0.0 copy-done.9
  65.6 0.0 copy-done.10
  65.6 0.0 copy-done.11
  65.7 7.1 %shard_map.147 = (bf16[8,256,128]{2,1,0:T(8,128)(2,1)}, f32[2304,256]{1,0:T(8,128)S(1)}, f32[2304,256]{1,0:T(8,128)S(1)}) custom-call(bf16[32,96,256]{2,1,0:T(8,128)(2,1)S(1)} %all_to_all.20.received, bf16[144,128]{1,0:T(8,128)(2,1)S(1)} %copy-done.14, f32[72,256]{1,0:T(8,128)S(1)} %copy-done.12, f32[72,256]{1,0:T(8,128)S(1)} %copy-done.11, ...), custom_call_target="tpu_custom_call" | custom-call | flops 5000000000 | bytes 8388608 | tf_op jit(solution)/shard_map/pallas_call | solution.py:314
  72.8 1.4 %copy-done.15 = f32[2304,256]{1,0:T(8,128)} copy-done((f32[2304,256]{1,0:T(8,128)}, f32[2304,256]{1,0:T(8,128)S(1)}, u32[]{:S(2)}) %copy-start.15) | copy-done | bytes 2359320
  74.2 1.4 copy-done.17
  75.7 0.0 all-to-all-done.1.taps
  75.7 5.7 %all-to-all-start.2 = ((bf16[8,256,128]{2,1,0:T(8,128)(2,1)}), bf16[8,256,128]{2,1,0:T(8,128)(2,1)}, u32[]{:S(2)}, u32[]{:S(2)}) async-start(bf16[8,256,128]{2,1,0:T(8,128)(2,1)} %get-tuple-element.22), calls=%async_computation.2 | async-start | bytes 1048576 | tf_op jit(solution)/shard_map/all_to_all | solution.py:356
  81.4 1.7 %copy-done.16 = f32[2304,256]{1,0:T(8,128)S(1)} copy-done((f32[2304,256]{1,0:T(8,128)S(1)}, f32[2304,256]{1,0:T(8,128)}, u32[]{:S(2)}) %copy-start.16) | copy-done | bytes 2359320
  83.0 1.7 %copy-done.18 = f32[2304,256]{1,0:T(8,128)S(1)} copy-done((f32[2304,256]{1,0:T(8,128)S(1)}, f32[2304,256]{1,0:T(8,128)}, u32[]{:S(2)}) %copy-start.18) | copy-done | bytes 2359320
  84.7 6.5 %shard_map.148 = bf16[32,96,256]{2,1,0:T(8,128)(2,1)S(1)} custom-call(bf16[8,256,128]{2,1,0:T(8,128)(2,1)S(1)} %all-to-all-done.1.taps, f32[2304,256]{1,0:T(8,128)S(1)} %copy-done.16, f32[2304,256]{1,0:T(8,128)S(1)} %copy-done.18, bf16[144,128]{1,0:T(8,128)(2,1)S(1)} %copy-done.14, f32[72,256]{1,0:T(8,128)S(1)} %copy-done.12, f32[72,256]{1,0:T(8,128)S(1)} %copy-done.11, ...), custom_call_target="tpu_custom_call" | custom-call | flops 5000000000 | bytes 8388608 | tf_op jit(solution)/shard_map/pallas_call | solution.py:332
  91.2 0.0 all-to-all-done.2
  91.2 1.1 bitcast_dynamic-update-slice_fusion
  92.4 0.0 copy-start.1
  92.4 0.0 copy-start.3
  92.4 0.0 copy-start.5
  92.4 0.0 copy-start.7
  92.4 46.5 %all_to_all.21.back = bf16[32,96,256]{2,1,0:T(8,128)(2,1)S(1)} all-to-all(bf16[32,96,256]{2,1,0:T(8,128)(2,1)S(1)} %bitcast_dynamic-update-slice_fusion), channel_id=1, replica_groups=mesh['ctx'=32,'tp'=8] {'ctx'}, dimensions={0} | all-to-all | bytes 3145728 | tf_op jit(solution)/shard_map/all_to_all | solution.py:360
  138.9 0.0 copy-done.5
  138.9 4.7 %shard_map.149 = (bf16[256,1024]{1,0:T(8,128)(2,1)}, bf16[256,1024]{1,0:T(8,128)(2,1)}, bf16[256,1024]{1,0:T(8,128)(2,1)}, bf16[256,1024]{1,0:T(8,128)(2,1)}, bf16[32,8192]{1,0:T(8,128)(2,1)}) custom-call(bf16[256,1024]{1,0:T(8,128)(2,1)S(1)} %copy-done.1, bf16[256,1024]{1,0:T(8,128)(2,1)S(1)} %copy-done.3, bf16[256,1024]{1,0:T(8,128)(2,1)S(1)} %copy-done.5, ...), custom_call_target="tpu_custom_call" | custom-call | flops 1000000 | bytes 6291456 | tf_op jit(solution)/shard_map/pallas_call | solution.py:292
  (19 shorter events, 0.1 us)
Async XLA Ops:
  0.6 1.0 copy-start
  1.7 1.0 copy-start.2
  2.7 1.0 copy-start.4
  3.8 1.0 copy-start.6
  4.8 1.0 copy-start.8
  58.9 6.7 %copy-start.9 = (bf16[768,256]{1,0:T(8,128)(2,1)S(1)}, bf16[768,256]{1,0:T(8,128)(2,1)}, u32[]{:S(2)}) copy-start(bf16[768,256]{1,0:T(8,128)(2,1)} %constant.45.clone.back) | copy-start | bytes 1179652
  58.9 6.7 %copy-start.10 = (bf16[768,256]{1,0:T(8,128)(2,1)S(1)}, bf16[768,256]{1,0:T(8,128)(2,1)}, u32[]{:S(2)}) copy-start(bf16[768,256]{1,0:T(8,128)(2,1)} %constant.44.clone.ahead) | copy-start | bytes 1179652
  58.9 6.7 %copy-start.11 = (f32[72,256]{1,0:T(8,128)S(1)}, f32[72,256]{1,0:T(8,128)}, u32[]{:S(2)}) copy-start(f32[72,256]{1,0:T(8,128)} %constant.43.clone.twist_imag) | copy-start | bytes 221188
  58.9 6.7 %copy-start.12 = (f32[72,256]{1,0:T(8,128)S(1)}, f32[72,256]{1,0:T(8,128)}, u32[]{:S(2)}) copy-start(f32[72,256]{1,0:T(8,128)} %constant.42.clone.twist_real) | copy-start | bytes 221188
  58.9 6.7 %copy-start.13 = (bf16[64,432]{1,0:T(8,128)(2,1)S(1)}, bf16[64,432]{1,0:T(8,128)(2,1)}, u32[]{:S(2)}) copy-start(bf16[64,432]{1,0:T(8,128)(2,1)} %constant.46.clone.last) | copy-start | bytes 165892
  59.0 6.7 %copy-start.14 = (bf16[144,128]{1,0:T(8,128)(2,1)S(1)}, bf16[144,128]{1,0:T(8,128)(2,1)}, u32[]{:S(2)}) copy-start(bf16[144,128]{1,0:T(8,128)(2,1)} %constant.41.clone.first) | copy-start | bytes 110596
  59.9 15.8 %all-to-all-start.1 = ((bf16[8,256,128]{2,1,0:T(8,128)(2,1)}), bf16[8,256,128]{2,1,0:T(8,128)(2,1)S(1)}, u32[]{:S(2)}, u32[]{:S(2)}) async-start(bf16[8,256,128]{2,1,0:T(8,128)(2,1)} %bitcast.10), calls=%async_computation.1 | async-start | bytes 1048576 | tf_op jit(solution)/shard_map/all_to_all | solution.py:352
  72.8 1.4 %copy-start.15 = (f32[2304,256]{1,0:T(8,128)}, f32[2304,256]{1,0:T(8,128)S(1)}, u32[]{:S(2)}) copy-start(f32[2304,256]{1,0:T(8,128)S(1)} %get-tuple-element.20.spec_x) | copy-start | bytes 7077892
  74.2 1.4 copy-start.17
  75.7 15.6 %all-to-all-start.2 = ((bf16[8,256,128]{2,1,0:T(8,128)(2,1)}), bf16[8,256,128]{2,1,0:T(8,128)(2,1)}, u32[]{:S(2)}, u32[]{:S(2)}) async-start(bf16[8,256,128]{2,1,0:T(8,128)(2,1)} %get-tuple-element.22), calls=%async_computation.2 | async-start | bytes 1048576 | tf_op jit(solution)/shard_map/all_to_all | solution.py:356
  81.4 1.7 %copy-start.16 = (f32[2304,256]{1,0:T(8,128)S(1)}, f32[2304,256]{1,0:T(8,128)}, u32[]{:S(2)}) copy-start(f32[2304,256]{1,0:T(8,128)} %copy-done.15) | copy-start | bytes 7077892
  83.0 1.7 %copy-start.18 = (f32[2304,256]{1,0:T(8,128)S(1)}, f32[2304,256]{1,0:T(8,128)}, u32[]{:S(2)}) copy-start(f32[2304,256]{1,0:T(8,128)} %copy-done.17) | copy-start | bytes 7077892
  92.4 46.5 %copy-start.1 = (bf16[256,1024]{1,0:T(8,128)(2,1)S(1)}, bf16[256,1024]{1,0:T(8,128)(2,1)}, u32[]{:S(2)}) copy-start(bf16[256,1024]{1,0:T(8,128)(2,1)} %query.3) | copy-start | bytes 1572868
  92.4 46.5 %copy-start.3 = (bf16[256,1024]{1,0:T(8,128)(2,1)S(1)}, bf16[256,1024]{1,0:T(8,128)(2,1)}, u32[]{:S(2)}) copy-start(bf16[256,1024]{1,0:T(8,128)(2,1)} %key.3) | copy-start | bytes 1572868
  92.4 46.5 %copy-start.5 = (bf16[256,1024]{1,0:T(8,128)(2,1)S(1)}, bf16[256,1024]{1,0:T(8,128)(2,1)}, u32[]{:S(2)}) copy-start(bf16[256,1024]{1,0:T(8,128)(2,1)} %value.3) | copy-start | bytes 1572868
  92.4 46.5 %copy-start.7 = (bf16[256,1024]{1,0:T(8,128)(2,1)S(1)}, bf16[256,1024]{1,0:T(8,128)(2,1)}, u32[]{:S(2)}) copy-start(bf16[256,1024]{1,0:T(8,128)(2,1)} %cotangent.3) | copy-start | bytes 1572868

commit v2 on v0

v2 whole, which is shorter than its diff:
```python
import functools
import math

import jax
import jax.numpy as jnp
import ml_dtypes
import numpy as np
from jax import lax
from jax.experimental import pallas as pl
from jax.experimental.pallas import tpu as pltpu
from jax.sharding import PartitionSpec as P

F32 = jnp.float32
BF16 = jnp.bfloat16
LANES = 128
KEPT = 72
MIB = 1 << 20
UNROLL = 8
UNROLL_PAIR = 16
CHUNK = 4
COLUMNS = 512


def split_table(table):
    high = table.astype(ml_dtypes.bfloat16)
    low = (table - high.astype(np.float64)).astype(ml_dtypes.bfloat16)
    return high, low


def make_tables(seq_len):
    radix = 2 * seq_len // LANES
    blocks = radix // 2
    total = 2 * seq_len
    kept = radix // 2 + 1
    order = np.concatenate([np.arange(0, blocks, 2), np.arange(1, blocks, 2)])
    k1 = np.arange(KEPT)
    live = (k1 < kept).astype(np.float64)
    turn = 2 * math.pi * np.outer(k1, order) / radix
    first = np.concatenate([np.cos(turn) * live[:, None], -np.sin(turn) * live[:, None]], 0)
    first_table = np.concatenate(split_table(first), 1)
    lane = np.arange(LANES)
    twist = 2 * math.pi * np.outer(k1, lane) / total
    twist_real = np.tile(np.cos(twist), (1, 2)).astype(np.float32)
    twist_imag = np.tile(-np.sin(twist), (1, 2)).astype(np.float32)
    inner = 2 * math.pi * np.outer(lane, lane) / LANES
    cos, sin = np.cos(inner), np.sin(inner)
    ahead = split_table(np.block([[cos, -sin], [sin, cos]]))
    ahead_table = np.concatenate([ahead[0], ahead[0], ahead[1]], 0)
    back = split_table(np.block([[cos, sin], [-sin, cos]]))
    back_table = np.concatenate([back[0], back[0], back[1]], 0)
    weight = np.where((k1 == 0) | (k1 == radix // 2), 1.0, 2.0) * live
    weight = weight * seq_len ** (-0.5) / total
    last = split_table(np.concatenate([np.cos(turn.T) * weight, -np.sin(turn.T) * weight], 1))
    last_table = np.concatenate([last[0], last[0], last[1]], 1)
    return first_table, twist_real, twist_imag, ahead_table, back_table, last_table


def split_value(value):
    high = value.astype(BF16)
    low = (value - high.astype(F32)).astype(BF16)
    return high, low


def swap_blocks(parts):
    block = lax.broadcasted_iota(jnp.int32, parts[0].shape, 1) // (LANES // 4)

    def exchange(parts, bit):
        upper = (block & bit) != 0
        shift = bit * (LANES // 4)
        new = list(parts)
        for low in range(4):
            if low & bit:
                continue
            high = low | bit
            new[low] = jnp.where(upper, pltpu.roll(parts[high], shift, 1), parts[low])
            new[high] = jnp.where(upper, parts[high], pltpu.roll(parts[low], LANES - shift, 1))
        return new

    return exchange(exchange(parts, 2), 1)


def pair_rows(left, right):
    low = lax.broadcasted_iota(jnp.int32, left.shape, 1) < 4
    return (
        jnp.where(low, left, pltpu.roll(right, 4, 1)),
        jnp.where(low, pltpu.roll(left, 4, 1), right),
    )


def gather_kernel(query, key, value, cotangent, taps, out):
    width = query.shape[1]
    channels = taps.shape[1]
    step = pl.program_id(0)

    def interleave(left, right):
        left, right = pair_rows(left.reshape(-1, 8, LANES), right.reshape(-1, 8, LANES))
        return jnp.stack([left, right], 1).reshape(-1, 8, LANES)

    def turn(array):
        turned = array.T
        return interleave(turned[:, :LANES], turned[:, LANES:])

    def turn_taps(part):
        def some(first):
            pieces = []
            for tp in range(first, 8, 2):
                start = tp * (channels // 8) + step * width + part * LANES
                pieces.append(taps[:, pl.ds(pl.multiple_of(start, LANES), LANES)])
            return jnp.concatenate(pieces, 0).astype(F32).T

        return interleave(some(0), some(1))

    for part in range(width // LANES):
        column = slice(part * LANES, (part + 1) * LANES)
        gated = key[:, column].astype(F32) * value[:, column].astype(F32)
        grad = cotangent[:, column].astype(F32) * query[:, column].astype(F32)
        whole = jnp.concatenate([turn(gated), turn(grad), turn_taps(part)], 1)
        rows = whole.shape[0] * 24
        out[part * rows : (part + 1) * rows, :] = whole.reshape(rows, LANES).astype(BF16)


def scatter_kernel(
    query, key, value, cotangent, back, block_output, grad_query, grad_key, grad_value, grad_filter
):
    width = query.shape[1]
    tap_rows, channels = grad_filter.shape
    step = pl.program_id(0)

    def separate(array):
        array = array.reshape(-1, 2, 8, LANES)
        left, right = pair_rows(array[:, 0], array[:, 1])
        return left.reshape(-1, LANES), right.reshape(-1, LANES)

    def turn(array):
        return jnp.concatenate(separate(array), 1).T

    for part in range(width // LANES):
        column = slice(part * LANES, (part + 1) * LANES)
        rows = LANES // 4 * 24
        whole = back[part * rows : (part + 1) * rows, :].astype(F32).reshape(-1, 24, LANES)
        convolved = turn(whole[:, :8])
        block_output[:, column] = (query[:, column].astype(F32) * convolved).astype(BF16)
        grad_query[:, column] = (cotangent[:, column].astype(F32) * convolved).astype(BF16)
        adjoint = turn(whole[:, 8:16])
        grad_key[:, column] = (adjoint * value[:, column].astype(F32)).astype(BF16)
        grad_value[:, column] = (adjoint * key[:, column].astype(F32)).astype(BF16)
        for first, taps in enumerate(separate(whole[:, 16:])):
            turned = taps.T.astype(BF16)
            for one in range(4):
                start = (2 * one + first) * (channels // 8) + step * width + part * LANES
                grad_filter[:, pl.ds(pl.multiple_of(start, LANES), LANES)] = turned[
                    one * tap_rows : (one + 1) * tap_rows
                ]


def long_kernel(
    received, first, twist_real, twist_imag, ahead, back, last, out,
    arrived, leaving, taps_even, taps_odd, grad_even, grad_odd,
    stage_x, stage_g, stage_h, spec_x, spec_g, spec_h,
):
    groups = 8
    sources = received.shape[0] // (groups * 24)
    tall = sources * 8
    whole = received[...].astype(F32).reshape(sources * groups, 24, LANES)
    arrived[...] = whole[:, :16].reshape(sources * groups * 16, LANES)
    taps = whole[:, 16:].reshape(sources, groups, 8, LANES)
    for half, holder in enumerate((taps_even, taps_odd)):
        swapped = swap_blocks([taps[:, 4 * half + q].reshape(tall, LANES) for q in range(4)])
        for one in range(4):
            holder[one * tall : (one + 1) * tall, :] = swapped[one]

    def lanes_of(array):
        return array[:, :LANES], array[:, LANES:]

    def beside(one, two):
        return jnp.concatenate([one, two], 1)

    def wide_dot(array, table):
        high, low = split_value(array)
        return jnp.dot(
            jnp.concatenate([high, low, high], 1), table[...], preferred_element_type=F32
        )

    def rows_of(channel, count=1):
        return pl.ds(pl.multiple_of(channel * KEPT, KEPT), count * KEPT)

    def spaced(channel, start):
        return pl.ds(channel // 4 * 16 + channel % 4 + start, sources, stride=groups * 16)

    def tapped(channel):
        return pl.ds(channel // 8 * tall + channel % 8, sources, stride=8)

    def forward(load, stage, spec):
        @pl.loop(0, groups * 2, unroll=UNROLL_PAIR)
        def _(pair):
            even_one, odd_one = load(2 * pair)
            even_two, odd_two = load(2 * pair + 1)
            both = jnp.concatenate(
                [beside(even_one, even_two), beside(odd_one, odd_two)], 0
            ).astype(BF16)
            turned = jnp.dot(
                first[...], jnp.concatenate([both, both], 0), preferred_element_type=F32
            )
            real, imag = turned[:KEPT], turned[KEPT:]
            new_real = lanes_of(real * twist_real[...] - imag * twist_imag[...])
            new_imag = lanes_of(imag * twist_real[...] + real * twist_imag[...])
            for which in range(2):
                stage[rows_of(2 * pair + which), :LANES] = new_real[which]
                stage[rows_of(2 * pair + which), LANES:] = new_imag[which]

        @pl.loop(0, groups * 4 // CHUNK, unroll=UNROLL)
        def _(step):
            at = rows_of(step * CHUNK, CHUNK)
            spec[at, :] = wide_dot(stage[at, :], ahead)

    def backward(left, right, sign, stage, store):
        @pl.loop(0, groups * 4 // CHUNK, unroll=UNROLL)
        def _(step):
            at = rows_of(step * CHUNK, CHUNK)
            left_real, left_imag = lanes_of(left[at, :])
            right_real, right_imag = lanes_of(right[at, :])
            right_imag = sign * right_imag
            turned = wide_dot(
                beside(
                    left_real * right_real - left_imag * right_imag,
                    left_real * right_imag + left_imag * right_real,
                ),
                back,
            )
            cos, sin = twist_real[:, :LANES], twist_imag[:, :LANES]
            for one in range(CHUNK):
                real, imag = lanes_of(turned[one * KEPT : (one + 1) * KEPT])
                stage[rows_of(step * CHUNK + one), :LANES] = real * cos + imag * sin
                stage[rows_of(step * CHUNK + one), LANES:] = imag * cos - real * sin

        @pl.loop(0, groups * 2, unroll=UNROLL_PAIR)
        def _(pair):
            one_real, one_imag = lanes_of(stage[rows_of(2 * pair), :])
            two_real, two_imag = lanes_of(stage[rows_of(2 * pair + 1), :])
            high, low = split_value(
                jnp.concatenate([beside(one_real, two_real), beside(one_imag, two_imag)], 0)
            )
            signal = jnp.dot(
                last[...], jnp.concatenate([high, low, high], 0), preferred_element_type=F32
            )
            for which, half in enumerate(lanes_of(signal)):
                store(2 * pair + which, half[:sources], half[sources:])

    def load_from(start):
        return lambda channel: (
            arrived[spaced(channel, start), :],
            arrived[spaced(channel, start + 4), :],
        )

    def store_at(start):
        def store(channel, even, odd):
            leaving[spaced(channel, start), :] = even
            leaving[spaced(channel, start + 4), :] = odd

        return store

    def load_taps(channel):
        return taps_even[tapped(channel), :], taps_odd[tapped(channel), :]

    def store_grad(channel, even, odd):
        grad_even[tapped(channel), :] = even
        grad_odd[tapped(channel), :] = odd

    forward(load_from(0), stage_x, spec_x)
    forward(load_from(8), stage_g, spec_g)
    forward(load_taps, stage_h, spec_h)
    backward(spec_g, spec_x, -1.0, stage_x, store_grad)
    backward(spec_h, spec_x, 1.0, stage_g, store_at(0))
    backward(spec_g, spec_h, -1.0, stage_h, store_at(8))

    pieces = []
    for holder in (grad_even, grad_odd):
        swapped = swap_blocks([holder[one * tall : (one + 1) * tall, :] for one in range(4)])
        pieces += [piece.reshape(sources, 8, LANES) for piece in swapped]
    grad = jnp.stack(pieces, 1).reshape(sources * groups, 8, LANES)
    made = jnp.concatenate([leaving[...].reshape(sources * groups, 16, LANES), grad], 1)
    out[...] = made.reshape(received.shape).astype(BF16)


def gather(query, key, value, cotangent, taps, ranks):
    positions, width = query.shape
    column = pl.BlockSpec((positions, COLUMNS), lambda i: (0, i))
    steps = width // COLUMNS
    return pl.pallas_call(
        gather_kernel,
        grid=(steps,),
        in_specs=[column] * 4 + [pl.BlockSpec(taps.shape, lambda i: (0, 0))],
        out_specs=pl.BlockSpec((ranks * 24 // steps, LANES), lambda i: (i, 0)),
        out_shape=jax.ShapeDtypeStruct((ranks * 24, LANES), BF16),
        compiler_params=pltpu.CompilerParams(vmem_limit_bytes=60 * MIB),
        cost_estimate=pl.CostEstimate(flops=10**6, bytes_accessed=4 * MIB, transcendentals=0),
    )(query, key, value, cotangent, taps)


def scatter(query, key, value, cotangent, back, taps_shape):
    positions, width = query.shape
    column = pl.BlockSpec((positions, COLUMNS), lambda i: (0, i))
    steps = width // COLUMNS
    return pl.pallas_call(
        scatter_kernel,
        grid=(steps,),
        in_specs=[column] * 4 + [pl.BlockSpec((back.shape[0] // steps, LANES), lambda i: (i, 0))],
        out_specs=[column] * 4 + [pl.BlockSpec(taps_shape, lambda i: (0, 0))],
        out_shape=[jax.ShapeDtypeStruct((positions, width), BF16)] * 4
        + [jax.ShapeDtypeStruct(taps_shape, BF16)],
        compiler_params=pltpu.CompilerParams(vmem_limit_bytes=24 * MIB),
        cost_estimate=pl.CostEstimate(flops=10**6, bytes_accessed=6 * MIB, transcendentals=0),
    )(query, key, value, cotangent, back)


def long_convolution(received, seq_len):
    tables = [jnp.asarray(table) for table in make_tables(seq_len)]
    ranks = received.shape[0] // 24
    plain = pltpu.VMEM((ranks * 16, LANES), F32)
    taps = pltpu.VMEM((ranks * 4, LANES), F32)
    spectra = pltpu.VMEM((32 * KEPT, 2 * LANES), F32)
    return pl.pallas_call(
        long_kernel,
        out_shape=jax.ShapeDtypeStruct(received.shape, BF16),
        scratch_shapes=[plain, plain, taps, taps, taps, taps] + [spectra] * 6,
        compiler_params=pltpu.CompilerParams(vmem_limit_bytes=40 * MIB),
        cost_estimate=pl.CostEstimate(flops=10**10, bytes_accessed=3 * MIB, transcendentals=0),
    )(received, *tables)


def local(query_proj, key_proj, value_proj, cotangent, filter_taps):
    everyone = ("ctx", "tp")
    ranks = lax.axis_size("ctx") * lax.axis_size("tp")
    seq_len = query_proj.shape[0] * lax.axis_size("ctx")
    sent = gather(query_proj, key_proj, value_proj, cotangent, filter_taps, ranks)
    received = lax.all_to_all(sent, everyone, split_axis=0, concat_axis=0, tiled=True)
    made = long_convolution(received, seq_len)
    back = lax.all_to_all(made, everyone, split_axis=0, concat_axis=0, tiled=True)
    return scatter(query_proj, key_proj, value_proj, cotangent, back, filter_taps.shape)


def solution(mesh):
    placed = (P("ctx", "tp"),) * 4 + (P(("ctx", "tp"), None),)
    return jax.shard_map(local, mesh=mesh, in_specs=placed, out_specs=placed, check_vma=False)
```

time: 167 us -> 127 us (0.76)
  Pallas kernels: 39.1 us -> 18.7 us
  blocking collectives: 123 us -> 106 us
  local copies, waits for them, and re-layouts: 2.11 us -> 0.06 us
    pallas_call x1, Pallas kernels: 33.3 us -> 13.2 us  [long_convolution(): pl.pallas_call(long_kernel, out_shape=jax.ShapeDtypeStruct(received.shape...]
    all_to_all x4 -> x2, blocking collectives: 123 us -> 106 us  [the longest x1 56.6 us: local(): lax.all_to_all(sent, everyone, split_axis=0, concat_axis=0, tiled=True)]
    all_to_all x2 -> x0, local copies, waits for them, and re-layouts: 2.05 us -> none  [the longest x1 1.22 us: local(): lax.all_to_all(filter_taps, 'tp', split_axis=1, concat_axis=0, tiled=True)]
where the time goes in v2:
time: 127 us; the launch traced here: 125 us
  blocking collectives  106 us (83%)
  Pallas kernels  18.7 us (15%)
    all_to_all x1, blocking collectives, local(): lax.all_to_all(sent, everyone, split_axis=0, concat_axis=0, tiled=True)  56.6 us
    all_to_all x1, blocking collectives, local(): lax.all_to_all(made, everyone, split_axis=0, concat_axis=0, tiled=True)  49 us
    pallas_call x1, Pallas kernels, long_convolution(): pl.pallas_call(long_kernel, out_shape=jax.ShapeDtypeStruct(received.shape...  13.2 us
    pallas_call x1, Pallas kernels, gather(): pl.pallas_call(gather_kernel, grid=(steps,), in_specs=[column] * 4 + [pl....  3.21 us

profile of v2, /device:TPU:34, one launch (start us, length us, event | category | flops | bytes accessed | tf_op | source)
XLA Modules:
  0.0 125.1 jit_solution(14211974737927848537)
XLA Ops:
  0.6 3.2 %shard_map.146 = bf16[6144,128]{1,0:T(8,128)(2,1)} custom-call(bf16[256,1024]{1,0:T(8,128)(2,1)} %query.3, bf16[256,1024]{1,0:T(8,128)(2,1)} %key.3, bf16[256,1024]{1,0:T(8,128)(2,1)} %value.3, bf16[256,1024]{1,0:T(8,128)(2,1)} %cotangent.3, bf16[32,8192]{1,0:T(8,128)(2,1)} %taps.1), custom_call_target="tpu_custom_call" | custom-call | flops 1000000 | bytes 4194304 | tf_op jit(solution)/shard_map/pallas_call | solution.py:289
  3.8 0.0 copy-start.4
  3.8 0.0 copy-start.5
  3.9 0.0 copy-start.6
  3.9 0.0 copy-start.7
  3.9 0.0 copy-start.8
  3.9 0.0 copy-start.9
  3.9 56.6 %all_to_all.22 = bf16[256,24,128]{2,1,0:T(8,128)(2,1)S(1)} all-to-all(bf16[256,24,128]{2,1,0:T(8,128)(2,1)} %bitcast.7), channel_id=1, replica_groups=mesh['ctx'=32,'tp'=8] {'ctx','tp'}, dimensions={0} | all-to-all | bytes 3145728 | tf_op jit(solution)/shard_map/all_to_all | solution.py:336
  60.5 0.0 copy-done.4
  60.5 0.0 copy-done.5
  60.5 0.0 copy-done.6
  60.5 0.0 copy-done.7
  60.5 0.0 copy-done.8
  60.6 0.0 copy-done.9
  60.6 13.2 %shard_map.147 = bf16[6144,128]{1,0:T(8,128)(2,1)S(1)} custom-call(bf16[6144,128]{1,0:T(8,128)(2,1)S(1)} %bitcast.5, bf16[144,128]{1,0:T(8,128)(2,1)S(1)} %copy-done.9, f32[72,256]{1,0:T(8,128)S(1)} %copy-done.7, f32[72,256]{1,0:T(8,128)S(1)} %copy-done.6, bf16[768,256]{1,0:T(8,128)(2,1)S(1)} %copy-done.5, bf16[768,256]{1,0:T(8,128)(2,1)S(1)} %copy-done.4, ...), custom_call_target="tpu_custom_call" | custom-call | flops 10000000000 | bytes 3145728 | tf_op jit(solution)/shard_map/pallas_call | solution.py:322
  73.8 0.0 copy-start
  73.8 0.0 copy-start.1
  73.8 0.0 copy-start.2
  73.8 0.0 copy-start.3
  73.8 49.0 %all_to_all.23 = bf16[256,24,128]{2,1,0:T(8,128)(2,1)S(1)} all-to-all(bf16[256,24,128]{2,1,0:T(8,128)(2,1)S(1)} %bitcast.6), channel_id=1, replica_groups=mesh['ctx'=32,'tp'=8] {'ctx','tp'}, dimensions={0} | all-to-all | bytes 3145728 | tf_op jit(solution)/shard_map/all_to_all | solution.py:338
  122.8 0.0 copy-done
  122.8 0.0 copy-done.1
  122.8 0.0 copy-done.2
  122.8 0.0 copy-done.3
  122.8 2.3 %shard_map.148 = (bf16[256,1024]{1,0:T(8,128)(2,1)}, bf16[256,1024]{1,0:T(8,128)(2,1)}, bf16[256,1024]{1,0:T(8,128)(2,1)}, bf16[256,1024]{1,0:T(8,128)(2,1)}, bf16[32,8192]{1,0:T(8,128)(2,1)}) custom-call(bf16[256,1024]{1,0:T(8,128)(2,1)S(1)} %copy-done, bf16[256,1024]{1,0:T(8,128)(2,1)S(1)} %copy-done.1, bf16[256,1024]{1,0:T(8,128)(2,1)S(1)} %copy-done.2, ...), custom_call_target="tpu_custom_call" | custom-call | flops 1000000 | bytes 6291456 | tf_op jit(solution)/shard_map/pallas_call | solution.py:304
Async XLA Ops:
  3.8 56.7 %copy-start.4 = (bf16[768,256]{1,0:T(8,128)(2,1)S(1)}, bf16[768,256]{1,0:T(8,128)(2,1)}, u32[]{:S(2)}) copy-start(bf16[768,256]{1,0:T(8,128)(2,1)} %constant.16.clone.back) | copy-start | bytes 1179652
  3.8 56.7 %copy-start.5 = (bf16[768,256]{1,0:T(8,128)(2,1)S(1)}, bf16[768,256]{1,0:T(8,128)(2,1)}, u32[]{:S(2)}) copy-start(bf16[768,256]{1,0:T(8,128)(2,1)} %constant.15.clone.ahead) | copy-start | bytes 1179652
  3.9 56.7 %copy-start.6 = (f32[72,256]{1,0:T(8,128)S(1)}, f32[72,256]{1,0:T(8,128)}, u32[]{:S(2)}) copy-start(f32[72,256]{1,0:T(8,128)} %constant.14.clone.twist_imag) | copy-start | bytes 221188
  3.9 56.7 %copy-start.7 = (f32[72,256]{1,0:T(8,128)S(1)}, f32[72,256]{1,0:T(8,128)}, u32[]{:S(2)}) copy-start(f32[72,256]{1,0:T(8,128)} %constant.13.clone.twist_real) | copy-start | bytes 221188
  3.9 56.7 %copy-start.8 = (bf16[64,432]{1,0:T(8,128)(2,1)S(1)}, bf16[64,432]{1,0:T(8,128)(2,1)}, u32[]{:S(2)}) copy-start(bf16[64,432]{1,0:T(8,128)(2,1)} %constant.17.clone.last) | copy-start | bytes 165892
  3.9 56.7 %copy-start.9 = (bf16[144,128]{1,0:T(8,128)(2,1)S(1)}, bf16[144,128]{1,0:T(8,128)(2,1)}, u32[]{:S(2)}) copy-start(bf16[144,128]{1,0:T(8,128)(2,1)} %constant.12.clone.first) | copy-start | bytes 110596
  73.8 49.0 %copy-start = (bf16[256,1024]{1,0:T(8,128)(2,1)S(1)}, bf16[256,1024]{1,0:T(8,128)(2,1)}, u32[]{:S(2)}) copy-start(bf16[256,1024]{1,0:T(8,128)(2,1)} %query.3) | copy-start | bytes 1572868
  73.8 49.0 %copy-start.1 = (bf16[256,1024]{1,0:T(8,128)(2,1)S(1)}, bf16[256,1024]{1,0:T(8,128)(2,1)}, u32[]{:S(2)}) copy-start(bf16[256,1024]{1,0:T(8,128)(2,1)} %key.3) | copy-start | bytes 1572868
  73.8 49.0 %copy-start.2 = (bf16[256,1024]{1,0:T(8,128)(2,1)S(1)}, bf16[256,1024]{1,0:T(8,128)(2,1)}, u32[]{:S(2)}) copy-start(bf16[256,1024]{1,0:T(8,128)(2,1)} %value.3) | copy-start | bytes 1572868
  73.8 49.0 %copy-start.3 = (bf16[256,1024]{1,0:T(8,128)(2,1)S(1)}, bf16[256,1024]{1,0:T(8,128)(2,1)}, u32[]{:S(2)}) copy-start(bf16[256,1024]{1,0:T(8,128)(2,1)} %cotangent.3) | copy-start | bytes 1572868

commit v3 on v2

v3 whole, which is shorter than its diff:
```python
import functools
import math

import jax
import jax.numpy as jnp
import ml_dtypes
import numpy as np
from jax import lax
from jax.experimental import pallas as pl
from jax.experimental.pallas import tpu as pltpu
from jax.sharding import PartitionSpec as P

F32 = jnp.float32
BF16 = jnp.bfloat16
LANES = 128
KEPT = 64
MIB = 1 << 20
PIECES = 2


def split_table(table):
    high = table.astype(ml_dtypes.bfloat16)
    low = (table - high.astype(np.float64)).astype(ml_dtypes.bfloat16)
    return high, low


def make_tables(seq_len):
    radix = 2 * seq_len // LANES
    blocks = radix // 2
    total = 2 * seq_len
    order = np.concatenate([np.arange(0, blocks, 2), np.arange(1, blocks, 2)])
    k1 = np.arange(KEPT)
    turn = 2 * math.pi * np.outer(k1, order) / radix
    middle = np.cos(math.pi * order)[None]
    first = np.concatenate([np.cos(turn), middle, -np.sin(turn[1:])], 0)
    first_table = np.concatenate(split_table(first), 1)
    lane = np.arange(LANES)
    twist = 2 * math.pi * np.outer(np.arange(KEPT + 1), lane) / total
    cos, sin = np.tile(np.cos(twist), (1, 2)), np.tile(-np.sin(twist), (1, 2))
    masked = np.where(k1[:, None] == 0, 0.0, cos[:KEPT])
    middle_twist = np.concatenate([cos[KEPT:], sin[KEPT:]], 0)
    twists = [table.astype(np.float32) for table in (cos[:KEPT], sin[:KEPT], masked, middle_twist)]
    inner = 2 * math.pi * np.outer(lane, lane) / LANES
    cos, sin = np.cos(inner), np.sin(inner)
    ahead = split_table(np.block([[cos, -sin], [sin, cos]]))
    ahead_table = np.concatenate([ahead[0], ahead[0], ahead[1]], 0)
    back = split_table(np.block([[cos, sin], [-sin, cos]]))
    back_table = np.concatenate([back[0], back[0], back[1]], 0)
    weight = np.where(k1 == 0, 1.0, 2.0)
    last = np.concatenate([np.cos(turn.T) * weight, middle.T, -2.0 * np.sin(turn[1:].T)], 1)
    high, low = split_table(last * (seq_len ** (-0.5) / total))
    last_table = np.block([[high, high], [low, np.zeros_like(low)]])
    return first_table, *twists, ahead_table, back_table, last_table


def split_value(value):
    high = value.astype(BF16)
    low = (value - high.astype(F32)).astype(BF16)
    return high, low


def swap_blocks(parts):
    block = lax.broadcasted_iota(jnp.int32, parts[0].shape, 1) // (LANES // 4)

    def exchange(parts, bit):
        upper = (block & bit) != 0
        shift = bit * (LANES // 4)
        new = list(parts)
        for low in range(4):
            if low & bit:
                continue
            high = low | bit
            new[low] = jnp.where(upper, pltpu.roll(parts[high], shift, 1), parts[low])
            new[high] = jnp.where(upper, parts[high], pltpu.roll(parts[low], LANES - shift, 1))
        return new

    return exchange(exchange(parts, 2), 1)


def pair_rows(left, right):
    low = lax.broadcasted_iota(jnp.int32, left.shape, 1) < 4
    return (
        jnp.where(low, left, pltpu.roll(right, 4, 1)),
        jnp.where(low, pltpu.roll(left, 4, 1), right),
    )


def gather_kernel(
    query, key, value, cotangent, taps, out, wide, taps_here, out_here, sems, taps_sem, out_sems
):
    pieces, _, _, width = wide.shape
    channels = taps.shape[1]
    rows = out.shape[0] // pieces

    def columns(piece):
        return pl.ds(piece * width, width)

    loads = [
        [
            pltpu.make_async_copy(
                array.at[:, columns(piece)], wide.at[piece, index], sems.at[piece, index]
            )
            for index, array in enumerate((key, value, cotangent, query))
        ]
        for piece in range(pieces)
    ]
    taps_load = pltpu.make_async_copy(taps, taps_here, taps_sem)
    stores = [
        pltpu.make_async_copy(
            out_here.at[pl.ds(piece * rows, rows)],
            out.at[pl.ds(piece * rows, rows)],
            out_sems.at[piece],
        )
        for piece in range(pieces)
    ]
    for piece in range(pieces):
        for load in loads[piece]:
            load.start()
        if piece == 0:
            taps_load.start()

    def interleave(left, right):
        left, right = pair_rows(left.reshape(-1, 8, LANES), right.reshape(-1, 8, LANES))
        return jnp.stack([left, right], 1).reshape(-1, 8, LANES)

    def turn(left, right):
        turned = (left.astype(F32) * right.astype(F32)).astype(BF16).T.astype(F32)
        return interleave(turned[:, :LANES], turned[:, LANES:])

    def turn_taps(start):
        def some(first):
            parts = []
            for tp in range(first, 8, 2):
                at = tp * (channels // 8) + start
                parts.append(taps_here[:, at : at + LANES])
            return jnp.concatenate(parts, 0).T.astype(F32)

        return interleave(some(0), some(1))

    for piece in range(pieces):
        for load in loads[piece]:
            load.wait()
        if piece == 0:
            taps_load.wait()
        for part in range(width // LANES):
            column = slice(part * LANES, (part + 1) * LANES)
            whole = jnp.concatenate(
                [
                    turn(wide[piece, 0, :, column], wide[piece, 1, :, column]),
                    turn(wide[piece, 2, :, column], wide[piece, 3, :, column]),
                    turn_taps(piece * width + part * LANES),
                ],
                1,
            )
            count = whole.shape[0] * 24
            at = piece * rows + part * count
            out_here[at : at + count, :] = whole.reshape(count, LANES).astype(BF16)
        stores[piece].start()
    for store in stores:
        store.wait()


def scatter_kernel(
    query, key, value, cotangent, back,
    block_output, grad_query, grad_key, grad_value, grad_filter,
    wide, taps_here, sems, taps_sem,
):
    pieces, _, _, width = wide.shape
    tap_rows, channels = grad_filter.shape
    rows = LANES // 4 * 24
    stores = [
        [
            pltpu.make_async_copy(
                wide.at[piece, index],
                array.at[:, pl.ds(piece * width, width)],
                sems.at[piece, index],
            )
            for index, array in enumerate((block_output, grad_query, grad_key, grad_value))
        ]
        for piece in range(pieces)
    ]
    taps_store = pltpu.make_async_copy(taps_here, grad_filter, taps_sem)

    def separate(array):
        array = array.reshape(-1, 2, 8, LANES)
        left, right = pair_rows(array[:, 0], array[:, 1])
        return left.reshape(-1, LANES), right.reshape(-1, LANES)

    def turn(array):
        return jnp.concatenate(separate(array), 1).astype(BF16).T.astype(F32)

    def arrived(block):
        return back[block * rows : (block + 1) * rows, :].astype(F32).reshape(-1, 24, LANES)

    for block in range(pieces * width // LANES):
        for first, taps in enumerate(separate(arrived(block)[:, 16:])):
            turned = taps.astype(BF16).T
            for one in range(4):
                at = (2 * one + first) * (channels // 8) + block * LANES
                taps_here[:, at : at + LANES] = turned[one * tap_rows : (one + 1) * tap_rows]
    taps_store.start()
    for piece in range(pieces):
        for start, factors in ((0, (query, cotangent)), (8, (value, key))):
            for part in range(width // LANES):
                block = piece * (width // LANES) + part
                column = slice(block * LANES, (block + 1) * LANES)
                signal = turn(arrived(block)[:, start : start + 8])
                for index, factor in enumerate(factors):
                    product = (factor[:, column].astype(F32) * signal).astype(BF16)
                    wide[piece, start // 4 + index, :, part * LANES : (part + 1) * LANES] = product
            for index in range(2):
                stores[piece][start // 4 + index].start()
    for piece in range(pieces):
        for store in stores[piece]:
            store.wait()
    taps_store.wait()


def long_kernel(
    received, first, twist_real, twist_imag, twist_masked, middle_twist, ahead, back, last, out,
    arrived_x, arrived_g, leaving_y, leaving_z, taps_even, taps_odd, grad_even, grad_odd, split, middles, spectra, weights,
):
    groups = 8
    channels = 32
    wide = 4
    main = channels * KEPT
    sources = received.shape[0] // (groups * 24)
    tall = sources * 8
    whole = received[...].astype(F32).reshape(sources * groups, 24, LANES)
    arrived_x[...] = whole[:, :8].reshape(sources * groups * 8, LANES)
    arrived_g[...] = whole[:, 8:16].reshape(sources * groups * 8, LANES)
    taps = whole[:, 16:].reshape(sources, groups, 8, LANES)
    for half, holder in enumerate((taps_even, taps_odd)):
        swapped = swap_blocks([taps[:, 4 * half + q].reshape(tall, LANES) for q in range(4)])
        for one in range(4):
            holder[one * tall : (one + 1) * tall, :] = swapped[one]

    def lanes_of(array):
        return array[:, :LANES], array[:, LANES:]

    def beside(one, two):
        return jnp.concatenate([one, two], 1)

    def wide_dot(high, low, table):
        return jnp.dot(
            jnp.concatenate([high, low, high], 1), table[...], preferred_element_type=F32
        )

    def spaced(channel, start):
        return pl.ds(channel // 4 * 8 + channel % 4 + start, sources, stride=groups * 8)

    def tapped(channel):
        return pl.ds(channel // 8 * tall + channel % 8, sources, stride=8)

    def load(which, channel):
        if which == 2:
            return taps_even[tapped(channel), :], taps_odd[tapped(channel), :]
        arrived = (arrived_x, arrived_g)[which]
        return arrived[spaced(channel, 0), :], arrived[spaced(channel, 4), :]

    def store(which, channel, even, odd):
        if which == 2:
            grad_even[tapped(channel), :] = even
            grad_odd[tapped(channel), :] = odd
        else:
            leaving = (leaving_y, leaving_z)[which]
            leaving[spaced(channel, 0), :] = even
            leaving[spaced(channel, 4), :] = odd

    def enter(which, pair):
        even_one, odd_one = load(which, 2 * pair)
        even_two, odd_two = load(which, 2 * pair + 1)
        both = jnp.concatenate([beside(even_one, even_two), beside(odd_one, odd_two)], 0)
        both = both.astype(BF16)
        turned = jnp.dot(
            first[...], jnp.concatenate([both, both], 0), preferred_element_type=F32
        )
        real, imag = turned[:KEPT], turned[KEPT:]
        middle = imag[:1]
        for part, array in enumerate(
            (
                real * twist_real[...] - imag * twist_imag[...],
                imag * twist_masked[...] + real * twist_imag[...],
            )
        ):
            column = slice(part * LANES, (part + 1) * LANES)
            extra = lanes_of(middle * middle_twist[part : part + 1, :])
            for level, piece in enumerate(split_value(array)):
                for one, half in enumerate(lanes_of(piece)):
                    row = (2 * pair + one) * KEPT
                    split[which, level, row : row + KEPT, column] = half
            for one in range(2):
                middles[which, 2 * pair + one : 2 * pair + one + 1, column] = extra[one]

    def transform(which, step):
        if step is None:
            high, low = split_value(middles[which])
            at = slice(main, main + channels)
        else:
            at = slice(step * wide * KEPT, (step + 1) * wide * KEPT)
            high, low = split[which, 0, at, :], split[which, 1, at, :]
        spectra[which, at, :] = wide_dot(high, low, ahead)

    factors = ((2, 0, 1.0), (1, 2, -1.0), (1, 0, -1.0))

    def product(which, step):
        left, right, sign = factors[which]
        if step is None:
            at = slice(main, main + channels)
        else:
            at = slice(step * wide * KEPT, (step + 1) * wide * KEPT)
        left_real, left_imag = lanes_of(spectra[left, at, :])
        right_real, right_imag = lanes_of(spectra[right, at, :])
        if sign > 0:
            real = left_real * right_real - left_imag * right_imag
            imag = left_imag * right_real + left_real * right_imag
        else:
            real = left_real * right_real + left_imag * right_imag
            imag = left_imag * right_real - left_real * right_imag
        turned = wide_dot(*split_value(beside(real, imag)), back)
        if step is None:
            real, imag = lanes_of(turned)
            cos, sin = middle_twist[:1, :LANES], middle_twist[1:, :LANES]
            middles[which, :, :LANES] = real * cos + imag * sin
            return
        cos, sin = twist_real[:, :LANES], twist_imag[:, :LANES]
        top = lax.broadcasted_iota(jnp.int32, (8, LANES), 0) == 0
        for one in range(wide):
            channel = step * wide + one
            real, imag = lanes_of(turned[one * KEPT : (one + 1) * KEPT])
            new_real = real * cos + imag * sin
            new_imag = imag * cos - real * sin
            middle = middles[which, channel : channel + 1, :LANES]
            new_imag = jnp.concatenate([jnp.where(top, middle, new_imag[:8]), new_imag[8:]], 0)
            column = slice(channel % 2 * LANES, (channel % 2 + 1) * LANES)
            for part, array in enumerate((new_real, new_imag)):
                for level, piece in enumerate(split_value(array)):
                    row = (channel // 2 * 4 + 2 * level + part) * KEPT
                    weights[which, row : row + KEPT, column] = piece

    def leave(which, pair):
        signal = jnp.dot(
            last[...], weights[which, pair * 4 * KEPT : (pair + 1) * 4 * KEPT, :],
            preferred_element_type=F32,
        )
        signal = signal[: 2 * sources] + signal[2 * sources :]
        for one, half in enumerate(lanes_of(signal)):
            store(which, 2 * pair + one, half[:sources], half[sources:])

    def run(*lines):
        longest = max(len(line) for line in lines)
        for index in range(longest):
            for line in lines:
                low, high = index * len(line) // longest, (index + 1) * len(line) // longest
                for task, *where in line[low:high]:
                    task(*where)

    pairs = range(channels // 2)
    steps = [None, *range(channels // wide)]

    def line(task, which):
        return [(task, which, place) for place in (pairs if task in (enter, leave) else steps)]

    run(line(enter, 0))
    run(line(transform, 0), line(enter, 1))
    run(line(transform, 1), line(enter, 2))
    run(line(transform, 2), line(product, 2))
    run(line(product, 0), line(leave, 2))
    run(line(product, 1), line(leave, 0))
    run(line(leave, 1))

    pieces = []
    for holder in (grad_even, grad_odd):
        swapped = swap_blocks([holder[one * tall : (one + 1) * tall, :] for one in range(4)])
        pieces += [piece.reshape(sources, 8, LANES) for piece in swapped]
    grad = jnp.stack(pieces, 1).reshape(sources * groups, 8, LANES)
    shape = (sources * groups, 8, LANES)
    made = jnp.concatenate([leaving_y[...].reshape(shape), leaving_z[...].reshape(shape), grad], 1)
    out[...] = made.reshape(received.shape).astype(BF16)


def gather(query, key, value, cotangent, taps, ranks):
    positions, width = query.shape
    pieces = PIECES
    anywhere = pl.BlockSpec(memory_space=pl.ANY)
    return pl.pallas_call(
        gather_kernel,
        in_specs=[anywhere] * 5,
        out_specs=anywhere,
        out_shape=jax.ShapeDtypeStruct((ranks * 24, LANES), BF16),
        scratch_shapes=[
            pltpu.VMEM((pieces, 4, positions, width // pieces), BF16),
            pltpu.VMEM(taps.shape, BF16),
            pltpu.VMEM((ranks * 24, LANES), BF16),
            pltpu.SemaphoreType.DMA((pieces, 4)),
            pltpu.SemaphoreType.DMA,
            pltpu.SemaphoreType.DMA((pieces,)),
        ],
        compiler_params=pltpu.CompilerParams(vmem_limit_bytes=60 * MIB),
        cost_estimate=pl.CostEstimate(flops=10**6, bytes_accessed=4 * MIB, transcendentals=0),
    )(query, key, value, cotangent, taps)


def scatter(query, key, value, cotangent, back, taps_shape):
    positions, width = query.shape
    pieces = PIECES
    anywhere = pl.BlockSpec(memory_space=pl.ANY)
    return pl.pallas_call(
        scatter_kernel,
        out_specs=[anywhere] * 5,
        out_shape=[jax.ShapeDtypeStruct((positions, width), BF16)] * 4
        + [jax.ShapeDtypeStruct(taps_shape, BF16)],
        scratch_shapes=[
            pltpu.VMEM((pieces, 4, positions, width // pieces), BF16),
            pltpu.VMEM(taps_shape, BF16),
            pltpu.SemaphoreType.DMA((pieces, 4)),
            pltpu.SemaphoreType.DMA,
        ],
        compiler_params=pltpu.CompilerParams(vmem_limit_bytes=24 * MIB),
        cost_estimate=pl.CostEstimate(flops=10**6, bytes_accessed=6 * MIB, transcendentals=0),
    )(query, key, value, cotangent, back)


def long_convolution(received, seq_len):
    tables = [jnp.asarray(table) for table in make_tables(seq_len)]
    ranks = received.shape[0] // 24
    plain = pltpu.VMEM((ranks * 8, LANES), F32)
    taps = pltpu.VMEM((ranks * 4, LANES), F32)
    pair_lanes = 2 * LANES
    return pl.pallas_call(
        long_kernel,
        out_shape=jax.ShapeDtypeStruct(received.shape, BF16),
        scratch_shapes=[plain] * 4 + [taps] * 4
        + [
            pltpu.VMEM((3, 2, 32 * KEPT, pair_lanes), BF16),
            pltpu.VMEM((3, 32, pair_lanes), F32),
            pltpu.VMEM((3, 32 * KEPT + 32, pair_lanes), F32),
            pltpu.VMEM((3, 64 * KEPT, pair_lanes), BF16),
        ],
        compiler_params=pltpu.CompilerParams(vmem_limit_bytes=40 * MIB),
        cost_estimate=pl.CostEstimate(flops=10**10, bytes_accessed=3 * MIB, transcendentals=0),
    )(received, *tables)


def local(query_proj, key_proj, value_proj, cotangent, filter_taps):
    everyone = ("ctx", "tp")
    ranks = lax.axis_size("ctx") * lax.axis_size("tp")
    seq_len = query_proj.shape[0] * lax.axis_size("ctx")
    sent = gather(query_proj, key_proj, value_proj, cotangent, filter_taps, ranks)
    received = lax.all_to_all(sent, everyone, split_axis=0, concat_axis=0, tiled=True)
    made = long_convolution(received, seq_len)
    back = lax.all_to_all(made, everyone, split_axis=0, concat_axis=0, tiled=True)
    return scatter(query_proj, key_proj, value_proj, cotangent, back, filter_taps.shape)


def solution(mesh):
    placed = (P("ctx", "tp"),) * 4 + (P(("ctx", "tp"), None),)
    return jax.shard_map(local, mesh=mesh, in_specs=placed, out_specs=placed, check_vma=False)
```

time: 127 us -> 124 us (0.976)
  Pallas kernels: 18.7 us -> 16.4 us
    pallas_call x1, Pallas kernels: 13.2 us -> 11.3 us  [long_convolution(): pl.pallas_call(long_kernel, out_shape=jax.ShapeDtypeStruct(received.shape...]
where the time goes in v3:
time: 124 us; the launch traced here: 123 us
  blocking collectives  106 us (85%)
  Pallas kernels  16.4 us (13%)
    all_to_all x1, blocking collectives, local(): lax.all_to_all(sent, everyone, split_axis=0, concat_axis=0, tiled=True)  56.6 us
    all_to_all x1, blocking collectives, local(): lax.all_to_all(made, everyone, split_axis=0, concat_axis=0, tiled=True)  49 us
    pallas_call x1, Pallas kernels, long_convolution(): pl.pallas_call(long_kernel, out_shape=jax.ShapeDtypeStruct(received.shape...  11.3 us
    pallas_call x1, Pallas kernels, gather(): pl.pallas_call(gather_kernel, in_specs=[anywhere] * 5, out_specs=anywhere...  3.28 us

profile of v3, /device:TPU:34, one launch (start us, length us, event | category | flops | bytes accessed | tf_op | source)
XLA Modules:
  0.0 122.9 jit_solution(3664876268754332767)
XLA Ops:
  0.6 3.3 %shard_map.164 = bf16[6144,128]{1,0:T(8,128)(2,1)} custom-call(bf16[256,1024]{1,0:T(8,128)(2,1)} %query.3, bf16[256,1024]{1,0:T(8,128)(2,1)} %key.3, bf16[256,1024]{1,0:T(8,128)(2,1)} %value.3, bf16[256,1024]{1,0:T(8,128)(2,1)} %cotangent.3, bf16[32,8192]{1,0:T(8,128)(2,1)} %taps.1), custom_call_target="tpu_custom_call" | custom-call | flops 1000000 | bytes 4194304 | tf_op jit(solution)/shard_map/pallas_call | solution.py:386
  3.9 0.0 copy-start.4
  3.9 0.0 copy-start.5
  3.9 0.0 copy-start.6
  4.0 0.0 copy-start.7
  4.0 0.0 copy-start.8
  4.0 0.0 copy-start.9
  4.0 0.0 copy-start.10
  4.0 0.0 copy-start.11
  4.0 56.6 %all_to_all.22 = bf16[256,24,128]{2,1,0:T(8,128)(2,1)S(1)} all-to-all(bf16[256,24,128]{2,1,0:T(8,128)(2,1)} %bitcast.7), channel_id=1, replica_groups=mesh['ctx'=32,'tp'=8] {'ctx','tp'}, dimensions={0} | all-to-all | bytes 3145728 | tf_op jit(solution)/shard_map/all_to_all | solution.py:450
  60.6 0.0 copy-done.4
  60.6 0.0 copy-done.5
  60.7 0.0 copy-done.6
  60.7 0.0 copy-done.7
  60.7 0.0 copy-done.8
  60.7 0.0 copy-done.9
  60.7 0.0 copy-done.10
  60.7 0.0 copy-done.11
  60.7 11.3 %shard_map.165 = bf16[6144,128]{1,0:T(8,128)(2,1)S(1)} custom-call(bf16[6144,128]{1,0:T(8,128)(2,1)S(1)} %bitcast.5, bf16[128,128]{1,0:T(8,128)(2,1)S(1)} %copy-done.10, f32[64,256]{1,0:T(8,128)S(1)} %copy-done.9, f32[64,256]{1,0:T(8,128)S(1)} %copy-done.8, f32[64,256]{1,0:T(8,128)S(1)} %copy-done.7, f32[2,256]{1,0:T(2,128)S(1)} %copy-done.11, ...), custom_call_target="tpu_custom_call" | custom-call | flops 10000000000 | bytes 3145728 | tf_op jit(solution)/shard_map/pallas_call | solution.py:430
  72.0 0.0 copy-start
  72.0 0.0 copy-start.1
  72.0 0.0 copy-start.2
  72.1 0.0 copy-start.3
  72.1 49.0 %all_to_all.23 = bf16[256,24,128]{2,1,0:T(8,128)(2,1)S(1)} all-to-all(bf16[256,24,128]{2,1,0:T(8,128)(2,1)S(1)} %bitcast.6), channel_id=1, replica_groups=mesh['ctx'=32,'tp'=8] {'ctx','tp'}, dimensions={0} | all-to-all | bytes 3145728 | tf_op jit(solution)/shard_map/all_to_all | solution.py:452
  121.1 0.0 copy-done
  121.1 0.0 copy-done.1
  121.1 0.0 copy-done.2
  121.1 0.0 copy-done.3
  121.1 1.8 %shard_map.166 = (bf16[256,1024]{1,0:T(8,128)(2,1)}, bf16[256,1024]{1,0:T(8,128)(2,1)}, bf16[256,1024]{1,0:T(8,128)(2,1)}, bf16[256,1024]{1,0:T(8,128)(2,1)}, bf16[32,8192]{1,0:T(8,128)(2,1)}) custom-call(bf16[256,1024]{1,0:T(8,128)(2,1)S(1)} %copy-done, bf16[256,1024]{1,0:T(8,128)(2,1)S(1)} %copy-done.1, bf16[256,1024]{1,0:T(8,128)(2,1)S(1)} %copy-done.2, ...), custom_call_target="tpu_custom_call" | custom-call | flops 1000000 | bytes 6291456 | tf_op jit(solution)/shard_map/pallas_call | solution.py:408
Async XLA Ops:
  3.9 56.7 %copy-start.4 = (bf16[768,256]{1,0:T(8,128)(2,1)S(1)}, bf16[768,256]{1,0:T(8,128)(2,1)}, u32[]{:S(2)}) copy-start(bf16[768,256]{1,0:T(8,128)(2,1)} %constant.22.clone.back) | copy-start | bytes 1179652
  3.9 56.7 %copy-start.5 = (bf16[768,256]{1,0:T(8,128)(2,1)S(1)}, bf16[768,256]{1,0:T(8,128)(2,1)}, u32[]{:S(2)}) copy-start(bf16[768,256]{1,0:T(8,128)(2,1)} %constant.21.clone.ahead) | copy-start | bytes 1179652
  3.9 56.7 %copy-start.6 = (bf16[128,256]{1,0:T(8,128)(2,1)S(1)}, bf16[128,256]{1,0:T(8,128)(2,1)}, u32[]{:S(2)}) copy-start(bf16[128,256]{1,0:T(8,128)(2,1)} %constant.23.clone.last) | copy-start | bytes 196612
  4.0 56.7 %copy-start.7 = (f32[64,256]{1,0:T(8,128)S(1)}, f32[64,256]{1,0:T(8,128)}, u32[]{:S(2)}) copy-start(f32[64,256]{1,0:T(8,128)} %constant.19.clone.twist_masked) | copy-start | bytes 196612
  4.0 56.7 %copy-start.8 = (f32[64,256]{1,0:T(8,128)S(1)}, f32[64,256]{1,0:T(8,128)}, u32[]{:S(2)}) copy-start(f32[64,256]{1,0:T(8,128)} %constant.18.clone.twist_imag) | copy-start | bytes 196612
  4.0 56.7 %copy-start.9 = (f32[64,256]{1,0:T(8,128)S(1)}, f32[64,256]{1,0:T(8,128)}, u32[]{:S(2)}) copy-start(f32[64,256]{1,0:T(8,128)} %constant.17.clone.twist_real) | copy-start | bytes 196612
  4.0 56.7 %copy-start.10 = (bf16[128,128]{1,0:T(8,128)(2,1)S(1)}, bf16[128,128]{1,0:T(8,128)(2,1)}, u32[]{:S(2)}) copy-start(bf16[128,128]{1,0:T(8,128)(2,1)} %constant.16.clone.first) | copy-start | bytes 98308
  4.0 56.7 %copy-start.11 = (f32[2,256]{1,0:T(2,128)S(1)}, f32[2,256]{1,0:T(2,128)}, u32[]{:S(2)}) copy-start(f32[2,256]{1,0:T(2,128)} %constant.20.clone.middle_twist) | copy-start | bytes 6148
  72.0 49.0 %copy-start = (bf16[256,1024]{1,0:T(8,128)(2,1)S(1)}, bf16[256,1024]{1,0:T(8,128)(2,1)}, u32[]{:S(2)}) copy-start(bf16[256,1024]{1,0:T(8,128)(2,1)} %query.3) | copy-start | bytes 1572868
  72.0 49.0 %copy-start.1 = (bf16[256,1024]{1,0:T(8,128)(2,1)S(1)}, bf16[256,1024]{1,0:T(8,128)(2,1)}, u32[]{:S(2)}) copy-start(bf16[256,1024]{1,0:T(8,128)(2,1)} %key.3) | copy-start | bytes 1572868
  72.0 49.0 %copy-start.2 = (bf16[256,1024]{1,0:T(8,128)(2,1)S(1)}, bf16[256,1024]{1,0:T(8,128)(2,1)}, u32[]{:S(2)}) copy-start(bf16[256,1024]{1,0:T(8,128)(2,1)} %value.3) | copy-start | bytes 1572868
  72.1 49.0 %copy-start.3 = (bf16[256,1024]{1,0:T(8,128)(2,1)S(1)}, bf16[256,1024]{1,0:T(8,128)(2,1)}, u32[]{:S(2)}) copy-start(bf16[256,1024]{1,0:T(8,128)(2,1)} %cotangent.3) | copy-start | bytes 1572868

commit v4 on v3

--- a/solution.py
+++ b/solution.py
@@ -227,13 +227,20 @@
     sources = received.shape[0] // (groups * 24)
     tall = sources * 8
     whole = received[...].astype(F32).reshape(sources * groups, 24, LANES)
-    arrived_x[...] = whole[:, :8].reshape(sources * groups * 8, LANES)
-    arrived_g[...] = whole[:, 8:16].reshape(sources * groups * 8, LANES)
-    taps = whole[:, 16:].reshape(sources, groups, 8, LANES)
+    tight = groups * 8
+    pitch = tight + 1
+    whole = whole.reshape(sources, groups, 24, LANES)
+    for source in range(sources):
+        at = slice(source * pitch, source * pitch + tight)
+        arrived_x[at, :] = whole[source, :, :8].reshape(tight, LANES)
+        arrived_g[at, :] = whole[source, :, 8:16].reshape(tight, LANES)
+    taps = whole[:, :, 16:]
     for half, holder in enumerate((taps_even, taps_odd)):
         swapped = swap_blocks([taps[:, 4 * half + q].reshape(tall, LANES) for q in range(4)])
         for one in range(4):
-            holder[one * tall : (one + 1) * tall, :] = swapped[one]
+            for source in range(sources):
+                at = (one * sources + source) * 9
+                holder[at : at + 8, :] = swapped[one][source * 8 : (source + 1) * 8]
 
     def lanes_of(array):
         return array[:, :LANES], array[:, LANES:]
@@ -247,10 +254,10 @@
         )
 
     def spaced(channel, start):
-        return pl.ds(channel // 4 * 8 + channel % 4 + start, sources, stride=groups * 8)
+        return pl.ds(channel // 4 * 8 + channel % 4 + start, sources, stride=pitch)
 
     def tapped(channel):
-        return pl.ds(channel // 8 * tall + channel % 8, sources, stride=8)
+        return pl.ds(channel // 8 * (sources * 9) + channel % 8, sources, stride=9)
 
     def load(which, channel):
         if which == 2:
@@ -369,14 +376,22 @@
     run(line(product, 1), line(leave, 0))
     run(line(leave, 1))
 
+    def loose(holder, first, count, size):
+        starts = [(first + index) * (size + 1) for index in range(count)]
+        return [holder[start : start + size, :] for start in starts]
+
     pieces = []
     for holder in (grad_even, grad_odd):
-        swapped = swap_blocks([holder[one * tall : (one + 1) * tall, :] for one in range(4)])
+        swapped = swap_blocks(
+            [jnp.concatenate(loose(holder, one * sources, sources, 8), 0) for one in range(4)]
+        )
         pieces += [piece.reshape(sources, 8, LANES) for piece in swapped]
     grad = jnp.stack(pieces, 1).reshape(sources * groups, 8, LANES)
-    shape = (sources * groups, 8, LANES)
-    made = jnp.concatenate([leaving_y[...].reshape(shape), leaving_z[...].reshape(shape), grad], 1)
-    out[...] = made.reshape(received.shape).astype(BF16)
+    made = [
+        jnp.concatenate(loose(holder, 0, sources, tight), 0).reshape(sources * groups, 8, LANES)
+        for holder in (leaving_y, leaving_z)
+    ]
+    out[...] = jnp.concatenate([*made, grad], 1).reshape(received.shape).astype(BF16)
 
 
 def gather(query, key, value, cotangent, taps, ranks):
@@ -424,8 +439,8 @@
 def long_convolution(received, seq_len):
     tables = [jnp.asarray(table) for table in make_tables(seq_len)]
     ranks = received.shape[0] // 24
-    plain = pltpu.VMEM((ranks * 8, LANES), F32)
-    taps = pltpu.VMEM((ranks * 4, LANES), F32)
+    plain = pltpu.VMEM((ranks // 8 * 65 + 7, LANES), F32)
+    taps = pltpu.VMEM((ranks // 2 * 9, LANES), F32)
     pair_lanes = 2 * LANES
     return pl.pallas_call(
         long_kernel,

time: 124 us -> 122 us (0.984)
  Pallas kernels: 16.4 us -> 14.1 us
    pallas_call x1, Pallas kernels: 11.3 us -> 9.07 us  [long_convolution(): pl.pallas_call(long_kernel, out_shape=jax.ShapeDtypeStruct(received.shape...]
where the time goes in v4:
time: 122 us; the launch traced here: 121 us
  blocking collectives  106 us (87%)
  Pallas kernels  14.1 us (12%)
    all_to_all x1, blocking collectives, local(): lax.all_to_all(sent, everyone, split_axis=0, concat_axis=0, tiled=True)  56.6 us
    all_to_all x1, blocking collectives, local(): lax.all_to_all(made, everyone, split_axis=0, concat_axis=0, tiled=True)  49 us
    pallas_call x1, Pallas kernels, long_convolution(): pl.pallas_call(long_kernel, out_shape=jax.ShapeDtypeStruct(received.shape...  9.07 us
    pallas_call x1, Pallas kernels, gather(): pl.pallas_call(gather_kernel, in_specs=[anywhere] * 5, out_specs=anywhere...  3.28 us

profile of v4, /device:TPU:34, one launch (start us, length us, event | category | flops | bytes accessed | tf_op | source)
XLA Modules:
  0.0 120.6 jit_solution(16327058063319583699)
XLA Ops:
  0.6 3.3 %shard_map.164 = bf16[6144,128]{1,0:T(8,128)(2,1)} custom-call(bf16[256,1024]{1,0:T(8,128)(2,1)} %query.3, bf16[256,1024]{1,0:T(8,128)(2,1)} %key.3, bf16[256,1024]{1,0:T(8,128)(2,1)} %value.3, bf16[256,1024]{1,0:T(8,128)(2,1)} %cotangent.3, bf16[32,8192]{1,0:T(8,128)(2,1)} %taps.1), custom_call_target="tpu_custom_call" | custom-call | flops 1000000 | bytes 4194304 | tf_op jit(solution)/shard_map/pallas_call | solution.py:401
  3.9 0.0 copy-start.4
  3.9 0.0 copy-start.5
  3.9 0.0 copy-start.6
  4.0 0.0 copy-start.7
  4.0 0.0 copy-start.8
  4.0 0.0 copy-start.9
  4.0 0.0 copy-start.10
  4.0 0.0 copy-start.11
  4.0 56.6 %all_to_all.22 = bf16[256,24,128]{2,1,0:T(8,128)(2,1)S(1)} all-to-all(bf16[256,24,128]{2,1,0:T(8,128)(2,1)} %bitcast.7), channel_id=1, replica_groups=mesh['ctx'=32,'tp'=8] {'ctx','tp'}, dimensions={0} | all-to-all | bytes 3145728 | tf_op jit(solution)/shard_map/all_to_all | solution.py:465
  60.6 0.0 copy-done.4
  60.6 0.0 copy-done.5
  60.7 0.0 copy-done.6
  60.7 0.0 copy-done.7
  60.7 0.0 copy-done.8
  60.7 0.0 copy-done.9
  60.7 0.0 copy-done.10
  60.7 0.0 copy-done.11
  60.7 9.1 %shard_map.165 = bf16[6144,128]{1,0:T(8,128)(2,1)S(1)} custom-call(bf16[6144,128]{1,0:T(8,128)(2,1)S(1)} %bitcast.5, bf16[128,128]{1,0:T(8,128)(2,1)S(1)} %copy-done.10, f32[64,256]{1,0:T(8,128)S(1)} %copy-done.9, f32[64,256]{1,0:T(8,128)S(1)} %copy-done.8, f32[64,256]{1,0:T(8,128)S(1)} %copy-done.7, f32[2,256]{1,0:T(2,128)S(1)} %copy-done.11, ...), custom_call_target="tpu_custom_call" | custom-call | flops 10000000000 | bytes 3145728 | tf_op jit(solution)/shard_map/pallas_call | solution.py:445
  69.8 0.0 copy-start
  69.8 0.0 copy-start.1
  69.8 0.0 copy-start.2
  69.8 0.0 copy-start.3
  69.8 49.0 %all_to_all.23 = bf16[256,24,128]{2,1,0:T(8,128)(2,1)S(1)} all-to-all(bf16[256,24,128]{2,1,0:T(8,128)(2,1)S(1)} %bitcast.6), channel_id=1, replica_groups=mesh['ctx'=32,'tp'=8] {'ctx','tp'}, dimensions={0} | all-to-all | bytes 3145728 | tf_op jit(solution)/shard_map/all_to_all | solution.py:467
  118.8 0.0 copy-done
  118.8 0.0 copy-done.1
  118.8 0.0 copy-done.2
  118.8 0.0 copy-done.3
  118.8 1.8 %shard_map.166 = (bf16[256,1024]{1,0:T(8,128)(2,1)}, bf16[256,1024]{1,0:T(8,128)(2,1)}, bf16[256,1024]{1,0:T(8,128)(2,1)}, bf16[256,1024]{1,0:T(8,128)(2,1)}, bf16[32,8192]{1,0:T(8,128)(2,1)}) custom-call(bf16[256,1024]{1,0:T(8,128)(2,1)S(1)} %copy-done, bf16[256,1024]{1,0:T(8,128)(2,1)S(1)} %copy-done.1, bf16[256,1024]{1,0:T(8,128)(2,1)S(1)} %copy-done.2, ...), custom_call_target="tpu_custom_call" | custom-call | flops 1000000 | bytes 6291456 | tf_op jit(solution)/shard_map/pallas_call | solution.py:423
Async XLA Ops:
  3.9 56.7 %copy-start.4 = (bf16[768,256]{1,0:T(8,128)(2,1)S(1)}, bf16[768,256]{1,0:T(8,128)(2,1)}, u32[]{:S(2)}) copy-start(bf16[768,256]{1,0:T(8,128)(2,1)} %constant.22.clone.back) | copy-start | bytes 1179652
  3.9 56.7 %copy-start.5 = (bf16[768,256]{1,0:T(8,128)(2,1)S(1)}, bf16[768,256]{1,0:T(8,128)(2,1)}, u32[]{:S(2)}) copy-start(bf16[768,256]{1,0:T(8,128)(2,1)} %constant.21.clone.ahead) | copy-start | bytes 1179652
  3.9 56.7 %copy-start.6 = (bf16[128,256]{1,0:T(8,128)(2,1)S(1)}, bf16[128,256]{1,0:T(8,128)(2,1)}, u32[]{:S(2)}) copy-start(bf16[128,256]{1,0:T(8,128)(2,1)} %constant.23.clone.last) | copy-start | bytes 196612
  4.0 56.7 %copy-start.7 = (f32[64,256]{1,0:T(8,128)S(1)}, f32[64,256]{1,0:T(8,128)}, u32[]{:S(2)}) copy-start(f32[64,256]{1,0:T(8,128)} %constant.19.clone.twist_masked) | copy-start | bytes 196612
  4.0 56.7 %copy-start.8 = (f32[64,256]{1,0:T(8,128)S(1)}, f32[64,256]{1,0:T(8,128)}, u32[]{:S(2)}) copy-start(f32[64,256]{1,0:T(8,128)} %constant.18.clone.twist_imag) | copy-start | bytes 196612
  4.0 56.7 %copy-start.9 = (f32[64,256]{1,0:T(8,128)S(1)}, f32[64,256]{1,0:T(8,128)}, u32[]{:S(2)}) copy-start(f32[64,256]{1,0:T(8,128)} %constant.17.clone.twist_real) | copy-start | bytes 196612
  4.0 56.7 %copy-start.10 = (bf16[128,128]{1,0:T(8,128)(2,1)S(1)}, bf16[128,128]{1,0:T(8,128)(2,1)}, u32[]{:S(2)}) copy-start(bf16[128,128]{1,0:T(8,128)(2,1)} %constant.16.clone.first) | copy-start | bytes 98308
  4.0 56.7 %copy-start.11 = (f32[2,256]{1,0:T(2,128)S(1)}, f32[2,256]{1,0:T(2,128)}, u32[]{:S(2)}) copy-start(f32[2,256]{1,0:T(2,128)} %constant.20.clone.middle_twist) | copy-start | bytes 6148
  69.8 49.0 %copy-start = (bf16[256,1024]{1,0:T(8,128)(2,1)S(1)}, bf16[256,1024]{1,0:T(8,128)(2,1)}, u32[]{:S(2)}) copy-start(bf16[256,1024]{1,0:T(8,128)(2,1)} %query.3) | copy-start | bytes 1572868
  69.8 49.0 %copy-start.1 = (bf16[256,1024]{1,0:T(8,128)(2,1)S(1)}, bf16[256,1024]{1,0:T(8,128)(2,1)}, u32[]{:S(2)}) copy-start(bf16[256,1024]{1,0:T(8,128)(2,1)} %key.3) | copy-start | bytes 1572868
  69.8 49.0 %copy-start.2 = (bf16[256,1024]{1,0:T(8,128)(2,1)S(1)}, bf16[256,1024]{1,0:T(8,128)(2,1)}, u32[]{:S(2)}) copy-start(bf16[256,1024]{1,0:T(8,128)(2,1)} %value.3) | copy-start | bytes 1572868
  69.8 49.0 %copy-start.3 = (bf16[256,1024]{1,0:T(8,128)(2,1)S(1)}, bf16[256,1024]{1,0:T(8,128)(2,1)}, u32[]{:S(2)}) copy-start(bf16[256,1024]{1,0:T(8,128)(2,1)} %cotangent.3) | copy-start | bytes 1572868

commit v5 on v4

--- a/solution.py
+++ b/solution.py
@@ -36,7 +36,7 @@
     first_table = np.concatenate(split_table(first), 1)
     lane = np.arange(LANES)
     twist = 2 * math.pi * np.outer(np.arange(KEPT + 1), lane) / total
-    cos, sin = np.tile(np.cos(twist), (1, 2)), np.tile(-np.sin(twist), (1, 2))
+    cos, sin = np.cos(twist), -np.sin(twist)
     masked = np.where(k1[:, None] == 0, 0.0, cos[:KEPT])
     middle_twist = np.concatenate([cos[KEPT:], sin[KEPT:]], 0)
     twists = [table.astype(np.float32) for table in (cos[:KEPT], sin[:KEPT], masked, middle_twist)]
@@ -282,22 +282,18 @@
         turned = jnp.dot(
             first[...], jnp.concatenate([both, both], 0), preferred_element_type=F32
         )
-        real, imag = turned[:KEPT], turned[KEPT:]
-        middle = imag[:1]
-        for part, array in enumerate(
-            (
-                real * twist_real[...] - imag * twist_imag[...],
-                imag * twist_masked[...] + real * twist_imag[...],
-            )
-        ):
-            column = slice(part * LANES, (part + 1) * LANES)
-            extra = lanes_of(middle * middle_twist[part : part + 1, :])
-            for level, piece in enumerate(split_value(array)):
-                for one, half in enumerate(lanes_of(piece)):
-                    row = (2 * pair + one) * KEPT
-                    split[which, level, row : row + KEPT, column] = half
-            for one in range(2):
-                middles[which, 2 * pair + one : 2 * pair + one + 1, column] = extra[one]
+        cos, sin, masked = twist_real[...], twist_imag[...], twist_masked[...]
+        for one, half in enumerate(lanes_of(turned)):
+            real, imag = half[:KEPT], half[KEPT:]
+            row = (2 * pair + one) * KEPT
+            parts = (real * cos - imag * sin, imag * masked + real * sin)
+            for part, array in enumerate(parts):
+                column = slice(part * LANES, (part + 1) * LANES)
+                for level, piece in enumerate(split_value(array)):
+                    split[which, level, row : row + KEPT, column] = piece
+                middles[which, 2 * pair + one : 2 * pair + one + 1, column] = (
+                    imag[:1] * middle_twist[part : part + 1, :]
+                )
 
     def transform(which, step):
         if step is None:
@@ -327,10 +323,10 @@
         turned = wide_dot(*split_value(beside(real, imag)), back)
         if step is None:
             real, imag = lanes_of(turned)
-            cos, sin = middle_twist[:1, :LANES], middle_twist[1:, :LANES]
+            cos, sin = middle_twist[:1, :], middle_twist[1:, :]
             middles[which, :, :LANES] = real * cos + imag * sin
             return
-        cos, sin = twist_real[:, :LANES], twist_imag[:, :LANES]
+        cos, sin = twist_real[...], twist_imag[...]
         top = lax.broadcasted_iota(jnp.int32, (8, LANES), 0) == 0
         for one in range(wide):
             channel = step * wide + one
@@ -369,11 +365,11 @@
         return [(task, which, place) for place in (pairs if task in (enter, leave) else steps)]
 
     run(line(enter, 0))
-    run(line(transform, 0), line(enter, 1))
-    run(line(transform, 1), line(enter, 2))
+    run(line(enter, 1), line(transform, 0))
+    run(line(enter, 2), line(transform, 1))
     run(line(transform, 2), line(product, 2))
-    run(line(product, 0), line(leave, 2))
-    run(line(product, 1), line(leave, 0))
+    run(line(leave, 2), line(product, 0))
+    run(line(leave, 0), line(product, 1))
     run(line(leave, 1))
 
     def loose(holder, first, count, size):
@@ -439,8 +435,8 @@
 def long_convolution(received, seq_len):
     tables = [jnp.asarray(table) for table in make_tables(seq_len)]
     ranks = received.shape[0] // 24
-    plain = pltpu.VMEM((ranks // 8 * 65 + 7, LANES), F32)
-    taps = pltpu.VMEM((ranks // 2 * 9, LANES), F32)
+    plain = pltpu.VMEM((ranks // 8 * 65 + 72, LANES), F32)
+    taps = pltpu.VMEM((ranks // 2 * 9 + 16, LANES), F32)
     pair_lanes = 2 * LANES
     return pl.pallas_call(
         long_kernel,

time: 122 us -> 122 us (level)
  no operation moved by 1% of the time
where the time goes in v5:
time: 122 us; the launch traced here: 121 us
  blocking collectives  106 us (87%)
  Pallas kernels  14.1 us (12%)
    all_to_all x1, blocking collectives, local(): lax.all_to_all(sent, everyone, split_axis=0, concat_axis=0, tiled=True)  56.6 us
    all_to_all x1, blocking collectives, local(): lax.all_to_all(made, everyone, split_axis=0, concat_axis=0, tiled=True)  49 us
    pallas_call x1, Pallas kernels, long_convolution(): pl.pallas_call(long_kernel, out_shape=jax.ShapeDtypeStruct(received.shape...  9.06 us
    pallas_call x1, Pallas kernels, gather(): pl.pallas_call(gather_kernel, in_specs=[anywhere] * 5, out_specs=anywhere...  3.28 us

profile of v5, /device:TPU:34, one launch (start us, length us, event | category | flops | bytes accessed | tf_op | source)
XLA Modules:
  0.0 120.6 jit_solution(12173562675365468201)
XLA Ops:
  0.6 3.3 %shard_map.164 = bf16[6144,128]{1,0:T(8,128)(2,1)} custom-call(bf16[256,1024]{1,0:T(8,128)(2,1)} %query.3, bf16[256,1024]{1,0:T(8,128)(2,1)} %key.3, bf16[256,1024]{1,0:T(8,128)(2,1)} %value.3, bf16[256,1024]{1,0:T(8,128)(2,1)} %cotangent.3, bf16[32,8192]{1,0:T(8,128)(2,1)} %taps.1), custom_call_target="tpu_custom_call" | custom-call | flops 1000000 | bytes 4194304 | tf_op jit(solution)/shard_map/pallas_call | solution.py:397
  3.9 0.0 copy-start.4
  3.9 0.0 copy-start.5
  3.9 0.0 copy-start.6
  4.0 0.0 copy-start.7
  4.0 0.0 copy-start.8
  4.0 0.0 copy-start.9
  4.0 0.0 copy-start.10
  4.0 0.0 copy-start.11
  4.0 56.6 %all_to_all.22 = bf16[256,24,128]{2,1,0:T(8,128)(2,1)S(1)} all-to-all(bf16[256,24,128]{2,1,0:T(8,128)(2,1)} %bitcast.7), channel_id=1, replica_groups=mesh['ctx'=32,'tp'=8] {'ctx','tp'}, dimensions={0} | all-to-all | bytes 3145728 | tf_op jit(solution)/shard_map/all_to_all | solution.py:461
  60.6 0.0 copy-done.4
  60.6 0.0 copy-done.5
  60.7 0.0 copy-done.6
  60.7 0.0 copy-done.7
  60.7 0.0 copy-done.8
  60.7 0.0 copy-done.9
  60.7 0.0 copy-done.10
  60.7 0.0 copy-done.11
  60.7 9.1 %shard_map.165 = bf16[6144,128]{1,0:T(8,128)(2,1)S(1)} custom-call(bf16[6144,128]{1,0:T(8,128)(2,1)S(1)} %bitcast.5, bf16[128,128]{1,0:T(8,128)(2,1)S(1)} %copy-done.10, f32[64,128]{1,0:T(8,128)S(1)} %copy-done.9, f32[64,128]{1,0:T(8,128)S(1)} %copy-done.8, f32[64,128]{1,0:T(8,128)S(1)} %copy-done.7, f32[2,128]{1,0:T(2,128)S(1)} %copy-done.11, ...), custom_call_target="tpu_custom_call" | custom-call | flops 10000000000 | bytes 3145728 | tf_op jit(solution)/shard_map/pallas_call | solution.py:441
  69.8 0.0 copy-start
  69.8 0.0 copy-start.1
  69.8 0.0 copy-start.2
  69.8 0.0 copy-start.3
  69.8 49.0 %all_to_all.23 = bf16[256,24,128]{2,1,0:T(8,128)(2,1)S(1)} all-to-all(bf16[256,24,128]{2,1,0:T(8,128)(2,1)S(1)} %bitcast.6), channel_id=1, replica_groups=mesh['ctx'=32,'tp'=8] {'ctx','tp'}, dimensions={0} | all-to-all | bytes 3145728 | tf_op jit(solution)/shard_map/all_to_all | solution.py:463
  118.8 0.0 copy-done
  118.8 0.0 copy-done.1
  118.8 0.0 copy-done.2
  118.8 0.0 copy-done.3
  118.8 1.8 %shard_map.166 = (bf16[256,1024]{1,0:T(8,128)(2,1)}, bf16[256,1024]{1,0:T(8,128)(2,1)}, bf16[256,1024]{1,0:T(8,128)(2,1)}, bf16[256,1024]{1,0:T(8,128)(2,1)}, bf16[32,8192]{1,0:T(8,128)(2,1)}) custom-call(bf16[256,1024]{1,0:T(8,128)(2,1)S(1)} %copy-done, bf16[256,1024]{1,0:T(8,128)(2,1)S(1)} %copy-done.1, bf16[256,1024]{1,0:T(8,128)(2,1)S(1)} %copy-done.2, ...), custom_call_target="tpu_custom_call" | custom-call | flops 1000000 | bytes 6291456 | tf_op jit(solution)/shard_map/pallas_call | solution.py:419
Async XLA Ops:
  3.9 56.7 %copy-start.4 = (bf16[768,256]{1,0:T(8,128)(2,1)S(1)}, bf16[768,256]{1,0:T(8,128)(2,1)}, u32[]{:S(2)}) copy-start(bf16[768,256]{1,0:T(8,128)(2,1)} %constant.22.clone.back) | copy-start | bytes 1179652
  3.9 56.7 %copy-start.5 = (bf16[768,256]{1,0:T(8,128)(2,1)S(1)}, bf16[768,256]{1,0:T(8,128)(2,1)}, u32[]{:S(2)}) copy-start(bf16[768,256]{1,0:T(8,128)(2,1)} %constant.21.clone.ahead) | copy-start | bytes 1179652
  3.9 56.7 %copy-start.6 = (bf16[128,256]{1,0:T(8,128)(2,1)S(1)}, bf16[128,256]{1,0:T(8,128)(2,1)}, u32[]{:S(2)}) copy-start(bf16[128,256]{1,0:T(8,128)(2,1)} %constant.23.clone.last) | copy-start | bytes 196612
  4.0 56.7 %copy-start.7 = (f32[64,128]{1,0:T(8,128)S(1)}, f32[64,128]{1,0:T(8,128)}, u32[]{:S(2)}) copy-start(f32[64,128]{1,0:T(8,128)} %constant.19.clone.twist_masked) | copy-start | bytes 98308
  4.0 56.7 %copy-start.8 = (f32[64,128]{1,0:T(8,128)S(1)}, f32[64,128]{1,0:T(8,128)}, u32[]{:S(2)}) copy-start(f32[64,128]{1,0:T(8,128)} %constant.18.clone.twist_imag) | copy-start | bytes 98308
  4.0 56.7 %copy-start.9 = (f32[64,128]{1,0:T(8,128)S(1)}, f32[64,128]{1,0:T(8,128)}, u32[]{:S(2)}) copy-start(f32[64,128]{1,0:T(8,128)} %constant.17.clone.twist_real) | copy-start | bytes 98308
  4.0 56.7 %copy-start.10 = (bf16[128,128]{1,0:T(8,128)(2,1)S(1)}, bf16[128,128]{1,0:T(8,128)(2,1)}, u32[]{:S(2)}) copy-start(bf16[128,128]{1,0:T(8,128)(2,1)} %constant.16.clone.first) | copy-start | bytes 98308
  4.0 56.7 %copy-start.11 = (f32[2,128]{1,0:T(2,128)S(1)}, f32[2,128]{1,0:T(2,128)}, u32[]{:S(2)}) copy-start(f32[2,128]{1,0:T(2,128)} %constant.20.clone.middle_twist) | copy-start | bytes 3076
  69.8 49.0 %copy-start = (bf16[256,1024]{1,0:T(8,128)(2,1)S(1)}, bf16[256,1024]{1,0:T(8,128)(2,1)}, u32[]{:S(2)}) copy-start(bf16[256,1024]{1,0:T(8,128)(2,1)} %query.3) | copy-start | bytes 1572868
  69.8 49.0 %copy-start.1 = (bf16[256,1024]{1,0:T(8,128)(2,1)S(1)}, bf16[256,1024]{1,0:T(8,128)(2,1)}, u32[]{:S(2)}) copy-start(bf16[256,1024]{1,0:T(8,128)(2,1)} %key.3) | copy-start | bytes 1572868
  69.8 49.0 %copy-start.2 = (bf16[256,1024]{1,0:T(8,128)(2,1)S(1)}, bf16[256,1024]{1,0:T(8,128)(2,1)}, u32[]{:S(2)}) copy-start(bf16[256,1024]{1,0:T(8,128)(2,1)} %value.3) | copy-start | bytes 1572868
  69.8 49.0 %copy-start.3 = (bf16[256,1024]{1,0:T(8,128)(2,1)S(1)}, bf16[256,1024]{1,0:T(8,128)(2,1)}, u32[]{:S(2)}) copy-start(bf16[256,1024]{1,0:T(8,128)(2,1)} %cotangent.3) | copy-start | bytes 1572868

commit v6 on v5

--- a/solution.py
+++ b/solution.py
@@ -90,7 +90,8 @@
 ):
     pieces, _, _, width = wide.shape
     channels = taps.shape[1]
-    rows = out.shape[0] // pieces
+    parts = width // LANES
+    rows = out.shape[0] // pieces // parts
 
     def columns(piece):
         return pl.ds(piece * width, width)
@@ -107,11 +108,11 @@
     taps_load = pltpu.make_async_copy(taps, taps_here, taps_sem)
     stores = [
         pltpu.make_async_copy(
-            out_here.at[pl.ds(piece * rows, rows)],
-            out.at[pl.ds(piece * rows, rows)],
-            out_sems.at[piece],
+            out_here.at[pl.ds(block * rows, rows)],
+            out.at[pl.ds(block * rows, rows)],
+            out_sems.at[block],
         )
-        for piece in range(pieces)
+        for block in range(pieces * parts)
     ]
     for piece in range(pieces):
         for load in loads[piece]:
@@ -142,7 +143,7 @@
             load.wait()
         if piece == 0:
             taps_load.wait()
-        for part in range(width // LANES):
+        for part in range(parts):
             column = slice(part * LANES, (part + 1) * LANES)
             whole = jnp.concatenate(
                 [
@@ -152,10 +153,9 @@
                 ],
                 1,
             )
-            count = whole.shape[0] * 24
-            at = piece * rows + part * count
-            out_here[at : at + count, :] = whole.reshape(count, LANES).astype(BF16)
-        stores[piece].start()
+            block = piece * parts + part
+            out_here[block * rows : (block + 1) * rows, :] = whole.reshape(rows, LANES).astype(BF16)
+            stores[block].start()
     for store in stores:
         store.wait()
 
@@ -222,7 +222,7 @@
 ):
     groups = 8
     channels = 32
-    wide = 4
+    wide = 8
     main = channels * KEPT
     sources = received.shape[0] // (groups * 24)
     tall = sources * 8
@@ -295,25 +295,36 @@
                     imag[:1] * middle_twist[part : part + 1, :]
                 )
 
+    def rows_of(step):
+        return slice(step * wide * KEPT, (step + 1) * wide * KEPT)
+
+    middle_rows = slice(main, main + channels)
+
     def transform(which, step):
-        if step is None:
-            high, low = split_value(middles[which])
-            at = slice(main, main + channels)
-        else:
-            at = slice(step * wide * KEPT, (step + 1) * wide * KEPT)
-            high, low = split[which, 0, at, :], split[which, 1, at, :]
-        spectra[which, at, :] = wide_dot(high, low, ahead)
+        at = rows_of(step)
+        high, low = split[which, 0, at, :], split[which, 1, at, :]
+        if step == 0:
+            extra = split_value(middles[which])
+            high = jnp.concatenate([high, extra[0]], 0)
+            low = jnp.concatenate([low, extra[1]], 0)
+        result = wide_dot(high, low, ahead)
+        spectra[which, at, :] = result[: wide * KEPT]
+        if step == 0:
+            spectra[which, middle_rows, :] = result[wide * KEPT :]
 
     factors = ((2, 0, 1.0), (1, 2, -1.0), (1, 0, -1.0))
 
     def product(which, step):
         left, right, sign = factors[which]
-        if step is None:
-            at = slice(main, main + channels)
-        else:
-            at = slice(step * wide * KEPT, (step + 1) * wide * KEPT)
-        left_real, left_imag = lanes_of(spectra[left, at, :])
-        right_real, right_imag = lanes_of(spectra[right, at, :])
+
+        def part_of(index):
+            whole = spectra[index, rows_of(step), :]
+            if step == 0:
+                whole = jnp.concatenate([whole, spectra[index, middle_rows, :]], 0)
+            return lanes_of(whole)
+
+        left_real, left_imag = part_of(left)
+        right_real, right_imag = part_of(right)
         if sign > 0:
             real = left_real * right_real - left_imag * right_imag
             imag = left_imag * right_real + left_real * right_imag
@@ -321,11 +332,10 @@
             real = left_real * right_real + left_imag * right_imag
             imag = left_imag * right_real - left_real * right_imag
         turned = wide_dot(*split_value(beside(real, imag)), back)
-        if step is None:
-            real, imag = lanes_of(turned)
+        if step == 0:
+            real, imag = lanes_of(turned[wide * KEPT :])
             cos, sin = middle_twist[:1, :], middle_twist[1:, :]
-            middles[which, :, :LANES] = real * cos + imag * sin
-            return
+            middles[3 + which, :, :LANES] = real * cos + imag * sin
         cos, sin = twist_real[...], twist_imag[...]
         top = lax.broadcasted_iota(jnp.int32, (8, LANES), 0) == 0
         for one in range(wide):
@@ -333,7 +343,7 @@
             real, imag = lanes_of(turned[one * KEPT : (one + 1) * KEPT])
             new_real = real * cos + imag * sin
             new_imag = imag * cos - real * sin
-            middle = middles[which, channel : channel + 1, :LANES]
+            middle = middles[3 + which, channel : channel + 1, :LANES]
             new_imag = jnp.concatenate([jnp.where(top, middle, new_imag[:8]), new_imag[8:]], 0)
             column = slice(channel % 2 * LANES, (channel % 2 + 1) * LANES)
             for part, array in enumerate((new_real, new_imag)):
@@ -359,7 +369,7 @@
                     task(*where)
 
     pairs = range(channels // 2)
-    steps = [None, *range(channels // wide)]
+    steps = range(channels // wide)
 
     def line(task, which):
         return [(task, which, place) for place in (pairs if task in (enter, leave) else steps)]
@@ -405,7 +415,7 @@
             pltpu.VMEM((ranks * 24, LANES), BF16),
             pltpu.SemaphoreType.DMA((pieces, 4)),
             pltpu.SemaphoreType.DMA,
-            pltpu.SemaphoreType.DMA((pieces,)),
+            pltpu.SemaphoreType.DMA((width // LANES,)),
         ],
         compiler_params=pltpu.CompilerParams(vmem_limit_bytes=60 * MIB),
         cost_estimate=pl.CostEstimate(flops=10**6, bytes_accessed=4 * MIB, transcendentals=0),
@@ -444,7 +454,7 @@
         scratch_shapes=[plain] * 4 + [taps] * 4
         + [
             pltpu.VMEM((3, 2, 32 * KEPT, pair_lanes), BF16),
-            pltpu.VMEM((3, 32, pair_lanes), F32),
+            pltpu.VMEM((6, 32, pair_lanes), F32),
             pltpu.VMEM((3, 32 * KEPT + 32, pair_lanes), F32),
             pltpu.VMEM((3, 64 * KEPT, pair_lanes), BF16),
         ],

time: 122 us -> 122 us (level)
  no operation moved by 1% of the time
where the time goes in v6:
time: 122 us; the launch traced here: 120 us
  blocking collectives  106 us (87%)
  Pallas kernels  13.5 us (11%)
    all_to_all x1, blocking collectives, local(): lax.all_to_all(sent, everyone, split_axis=0, concat_axis=0, tiled=True)  56.6 us
    all_to_all x1, blocking collectives, local(): lax.all_to_all(made, everyone, split_axis=0, concat_axis=0, tiled=True)  49 us
    pallas_call x1, Pallas kernels, long_convolution(): pl.pallas_call(long_kernel, out_shape=jax.ShapeDtypeStruct(received.shape...  8.56 us
    pallas_call x1, Pallas kernels, gather(): pl.pallas_call(gather_kernel, in_specs=[anywhere] * 5, out_specs=anywhere...  3.15 us

profile of v6, /device:TPU:34, one launch (start us, length us, event | category | flops | bytes accessed | tf_op | source)
XLA Modules:
  0.0 120.0 jit_solution(9403021580729507938)
XLA Ops:
  0.6 3.1 %shard_map.164 = bf16[6144,128]{1,0:T(8,128)(2,1)} custom-call(bf16[256,1024]{1,0:T(8,128)(2,1)} %query.3, bf16[256,1024]{1,0:T(8,128)(2,1)} %key.3, bf16[256,1024]{1,0:T(8,128)(2,1)} %value.3, bf16[256,1024]{1,0:T(8,128)(2,1)} %cotangent.3, bf16[32,8192]{1,0:T(8,128)(2,1)} %taps.1), custom_call_target="tpu_custom_call" | custom-call | flops 1000000 | bytes 4194304 | tf_op jit(solution)/shard_map/pallas_call | solution.py:407
  3.8 0.0 copy-start.4
  3.8 0.0 copy-start.5
  3.8 0.0 copy-start.6
  3.8 0.0 copy-start.7
  3.8 0.0 copy-start.8
  3.8 0.0 copy-start.9
  3.9 0.0 copy-start.10
  3.9 0.0 copy-start.11
  3.9 56.6 %all_to_all.22 = bf16[256,24,128]{2,1,0:T(8,128)(2,1)S(1)} all-to-all(bf16[256,24,128]{2,1,0:T(8,128)(2,1)} %bitcast.7), channel_id=1, replica_groups=mesh['ctx'=32,'tp'=8] {'ctx','tp'}, dimensions={0} | all-to-all | bytes 3145728 | tf_op jit(solution)/shard_map/all_to_all | solution.py:471
  60.5 0.0 copy-done.4
  60.5 0.0 copy-done.5
  60.5 0.0 copy-done.6
  60.5 0.0 copy-done.7
  60.5 0.0 copy-done.8
  60.5 0.0 copy-done.9
  60.5 0.0 copy-done.10
  60.6 0.0 copy-done.11
  60.6 8.6 %shard_map.165 = bf16[6144,128]{1,0:T(8,128)(2,1)S(1)} custom-call(bf16[6144,128]{1,0:T(8,128)(2,1)S(1)} %bitcast.5, bf16[128,128]{1,0:T(8,128)(2,1)S(1)} %copy-done.10, f32[64,128]{1,0:T(8,128)S(1)} %copy-done.9, f32[64,128]{1,0:T(8,128)S(1)} %copy-done.8, f32[64,128]{1,0:T(8,128)S(1)} %copy-done.7, f32[2,128]{1,0:T(2,128)S(1)} %copy-done.11, ...), custom_call_target="tpu_custom_call" | custom-call | flops 10000000000 | bytes 3145728 | tf_op jit(solution)/shard_map/pallas_call | solution.py:451
  69.1 0.0 copy-start
  69.1 0.0 copy-start.1
  69.2 0.0 copy-start.2
  69.2 0.0 copy-start.3
  69.2 49.0 %all_to_all.23 = bf16[256,24,128]{2,1,0:T(8,128)(2,1)S(1)} all-to-all(bf16[256,24,128]{2,1,0:T(8,128)(2,1)S(1)} %bitcast.6), channel_id=1, replica_groups=mesh['ctx'=32,'tp'=8] {'ctx','tp'}, dimensions={0} | all-to-all | bytes 3145728 | tf_op jit(solution)/shard_map/all_to_all | solution.py:473
  118.2 0.0 copy-done
  118.2 0.0 copy-done.1
  118.2 0.0 copy-done.2
  118.2 0.0 copy-done.3
  118.2 1.8 %shard_map.166 = (bf16[256,1024]{1,0:T(8,128)(2,1)}, bf16[256,1024]{1,0:T(8,128)(2,1)}, bf16[256,1024]{1,0:T(8,128)(2,1)}, bf16[256,1024]{1,0:T(8,128)(2,1)}, bf16[32,8192]{1,0:T(8,128)(2,1)}) custom-call(bf16[256,1024]{1,0:T(8,128)(2,1)S(1)} %copy-done, bf16[256,1024]{1,0:T(8,128)(2,1)S(1)} %copy-done.1, bf16[256,1024]{1,0:T(8,128)(2,1)S(1)} %copy-done.2, ...), custom_call_target="tpu_custom_call" | custom-call | flops 1000000 | bytes 6291456 | tf_op jit(solution)/shard_map/pallas_call | solution.py:429
Async XLA Ops:
  3.8 56.7 %copy-start.4 = (bf16[768,256]{1,0:T(8,128)(2,1)S(1)}, bf16[768,256]{1,0:T(8,128)(2,1)}, u32[]{:S(2)}) copy-start(bf16[768,256]{1,0:T(8,128)(2,1)} %constant.22.clone.back) | copy-start | bytes 1179652
  3.8 56.7 %copy-start.5 = (bf16[768,256]{1,0:T(8,128)(2,1)S(1)}, bf16[768,256]{1,0:T(8,128)(2,1)}, u32[]{:S(2)}) copy-start(bf16[768,256]{1,0:T(8,128)(2,1)} %constant.21.clone.ahead) | copy-start | bytes 1179652
  3.8 56.7 %copy-start.6 = (bf16[128,256]{1,0:T(8,128)(2,1)S(1)}, bf16[128,256]{1,0:T(8,128)(2,1)}, u32[]{:S(2)}) copy-start(bf16[128,256]{1,0:T(8,128)(2,1)} %constant.23.clone.last) | copy-start | bytes 196612
  3.8 56.7 %copy-start.7 = (f32[64,128]{1,0:T(8,128)S(1)}, f32[64,128]{1,0:T(8,128)}, u32[]{:S(2)}) copy-start(f32[64,128]{1,0:T(8,128)} %constant.19.clone.twist_masked) | copy-start | bytes 98308
  3.8 56.7 %copy-start.8 = (f32[64,128]{1,0:T(8,128)S(1)}, f32[64,128]{1,0:T(8,128)}, u32[]{:S(2)}) copy-start(f32[64,128]{1,0:T(8,128)} %constant.18.clone.twist_imag) | copy-start | bytes 98308
  3.8 56.7 %copy-start.9 = (f32[64,128]{1,0:T(8,128)S(1)}, f32[64,128]{1,0:T(8,128)}, u32[]{:S(2)}) copy-start(f32[64,128]{1,0:T(8,128)} %constant.17.clone.twist_real) | copy-start | bytes 98308
  3.9 56.7 %copy-start.10 = (bf16[128,128]{1,0:T(8,128)(2,1)S(1)}, bf16[128,128]{1,0:T(8,128)(2,1)}, u32[]{:S(2)}) copy-start(bf16[128,128]{1,0:T(8,128)(2,1)} %constant.16.clone.first) | copy-start | bytes 98308
  3.9 56.7 %copy-start.11 = (f32[2,128]{1,0:T(2,128)S(1)}, f32[2,128]{1,0:T(2,128)}, u32[]{:S(2)}) copy-start(f32[2,128]{1,0:T(2,128)} %constant.20.clone.middle_twist) | copy-start | bytes 3076
  69.1 49.0 %copy-start = (bf16[256,1024]{1,0:T(8,128)(2,1)S(1)}, bf16[256,1024]{1,0:T(8,128)(2,1)}, u32[]{:S(2)}) copy-start(bf16[256,1024]{1,0:T(8,128)(2,1)} %query.3) | copy-start | bytes 1572868
  69.1 49.0 %copy-start.1 = (bf16[256,1024]{1,0:T(8,128)(2,1)S(1)}, bf16[256,1024]{1,0:T(8,128)(2,1)}, u32[]{:S(2)}) copy-start(bf16[256,1024]{1,0:T(8,128)(2,1)} %key.3) | copy-start | bytes 1572868
  69.2 49.0 %copy-start.2 = (bf16[256,1024]{1,0:T(8,128)(2,1)S(1)}, bf16[256,1024]{1,0:T(8,128)(2,1)}, u32[]{:S(2)}) copy-start(bf16[256,1024]{1,0:T(8,128)(2,1)} %value.3) | copy-start | bytes 1572868
  69.2 49.0 %copy-start.3 = (bf16[256,1024]{1,0:T(8,128)(2,1)S(1)}, bf16[256,1024]{1,0:T(8,128)(2,1)}, u32[]{:S(2)}) copy-start(bf16[256,1024]{1,0:T(8,128)(2,1)} %cotangent.3) | copy-start | bytes 1572868

commit v7 on v6

--- a/solution.py
+++ b/solution.py
@@ -378,9 +378,9 @@
     run(line(enter, 1), line(transform, 0))
     run(line(enter, 2), line(transform, 1))
     run(line(transform, 2), line(product, 2))
-    run(line(leave, 2), line(product, 0))
-    run(line(leave, 0), line(product, 1))
-    run(line(leave, 1))
+    run(line(product, 0))
+    run(line(leave, 2), line(product, 1))
+    run(line(leave, 0), line(leave, 1))
 
     def loose(holder, first, count, size):
         starts = [(first + index) * (size + 1) for index in range(count)]

time: 122 us -> 122 us (level)
  no operation moved by 1% of the time
where the time goes in v7:
time: 122 us; the launch traced here: 120 us
  blocking collectives  106 us (87%)
  Pallas kernels  13.5 us (11%)
    all_to_all x1, blocking collectives, local(): lax.all_to_all(sent, everyone, split_axis=0, concat_axis=0, tiled=True)  56.6 us
    all_to_all x1, blocking collectives, local(): lax.all_to_all(made, everyone, split_axis=0, concat_axis=0, tiled=True)  49 us
    pallas_call x1, Pallas kernels, long_convolution(): pl.pallas_call(long_kernel, out_shape=jax.ShapeDtypeStruct(received.shape...  8.51 us
    pallas_call x1, Pallas kernels, gather(): pl.pallas_call(gather_kernel, in_specs=[anywhere] * 5, out_specs=anywhere...  3.15 us

profile of v7, /device:TPU:34, one launch (start us, length us, event | category | flops | bytes accessed | tf_op | source)
XLA Modules:
  0.0 119.9 jit_solution(18272681232324382374)
XLA Ops:
  0.6 3.1 %shard_map.164 = bf16[6144,128]{1,0:T(8,128)(2,1)} custom-call(bf16[256,1024]{1,0:T(8,128)(2,1)} %query.3, bf16[256,1024]{1,0:T(8,128)(2,1)} %key.3, bf16[256,1024]{1,0:T(8,128)(2,1)} %value.3, bf16[256,1024]{1,0:T(8,128)(2,1)} %cotangent.3, bf16[32,8192]{1,0:T(8,128)(2,1)} %taps.1), custom_call_target="tpu_custom_call" | custom-call | flops 1000000 | bytes 4194304 | tf_op jit(solution)/shard_map/pallas_call | solution.py:407
  3.8 0.0 copy-start.4
  3.8 0.0 copy-start.5
  3.8 0.0 copy-start.6
  3.8 0.0 copy-start.7
  3.8 0.0 copy-start.8
  3.8 0.0 copy-start.9
  3.9 0.0 copy-start.10
  3.9 0.0 copy-start.11
  3.9 56.6 %all_to_all.22 = bf16[256,24,128]{2,1,0:T(8,128)(2,1)S(1)} all-to-all(bf16[256,24,128]{2,1,0:T(8,128)(2,1)} %bitcast.7), channel_id=1, replica_groups=mesh['ctx'=32,'tp'=8] {'ctx','tp'}, dimensions={0} | all-to-all | bytes 3145728 | tf_op jit(solution)/shard_map/all_to_all | solution.py:471
  60.5 0.0 copy-done.4
  60.5 0.0 copy-done.5
  60.5 0.0 copy-done.6
  60.5 0.0 copy-done.7
  60.5 0.0 copy-done.8
  60.5 0.0 copy-done.9
  60.5 0.0 copy-done.10
  60.6 0.0 copy-done.11
  60.6 8.5 %shard_map.165 = bf16[6144,128]{1,0:T(8,128)(2,1)S(1)} custom-call(bf16[6144,128]{1,0:T(8,128)(2,1)S(1)} %bitcast.5, bf16[128,128]{1,0:T(8,128)(2,1)S(1)} %copy-done.10, f32[64,128]{1,0:T(8,128)S(1)} %copy-done.9, f32[64,128]{1,0:T(8,128)S(1)} %copy-done.8, f32[64,128]{1,0:T(8,128)S(1)} %copy-done.7, f32[2,128]{1,0:T(2,128)S(1)} %copy-done.11, ...), custom_call_target="tpu_custom_call" | custom-call | flops 10000000000 | bytes 3145728 | tf_op jit(solution)/shard_map/pallas_call | solution.py:451
  69.1 0.0 copy-start
  69.1 0.0 copy-start.1
  69.1 0.0 copy-start.2
  69.1 0.0 copy-start.3
  69.1 49.0 %all_to_all.23 = bf16[256,24,128]{2,1,0:T(8,128)(2,1)S(1)} all-to-all(bf16[256,24,128]{2,1,0:T(8,128)(2,1)S(1)} %bitcast.6), channel_id=1, replica_groups=mesh['ctx'=32,'tp'=8] {'ctx','tp'}, dimensions={0} | all-to-all | bytes 3145728 | tf_op jit(solution)/shard_map/all_to_all | solution.py:473
  118.1 0.0 copy-done
  118.1 0.0 copy-done.1
  118.1 0.0 copy-done.2
  118.1 0.0 copy-done.3
  118.2 1.8 %shard_map.166 = (bf16[256,1024]{1,0:T(8,128)(2,1)}, bf16[256,1024]{1,0:T(8,128)(2,1)}, bf16[256,1024]{1,0:T(8,128)(2,1)}, bf16[256,1024]{1,0:T(8,128)(2,1)}, bf16[32,8192]{1,0:T(8,128)(2,1)}) custom-call(bf16[256,1024]{1,0:T(8,128)(2,1)S(1)} %copy-done, bf16[256,1024]{1,0:T(8,128)(2,1)S(1)} %copy-done.1, bf16[256,1024]{1,0:T(8,128)(2,1)S(1)} %copy-done.2, ...), custom_call_target="tpu_custom_call" | custom-call | flops 1000000 | bytes 6291456 | tf_op jit(solution)/shard_map/pallas_call | solution.py:429
Async XLA Ops:
  3.8 56.7 %copy-start.4 = (bf16[768,256]{1,0:T(8,128)(2,1)S(1)}, bf16[768,256]{1,0:T(8,128)(2,1)}, u32[]{:S(2)}) copy-start(bf16[768,256]{1,0:T(8,128)(2,1)} %constant.22.clone.back) | copy-start | bytes 1179652
  3.8 56.7 %copy-start.5 = (bf16[768,256]{1,0:T(8,128)(2,1)S(1)}, bf16[768,256]{1,0:T(8,128)(2,1)}, u32[]{:S(2)}) copy-start(bf16[768,256]{1,0:T(8,128)(2,1)} %constant.21.clone.ahead) | copy-start | bytes 1179652
  3.8 56.7 %copy-start.6 = (bf16[128,256]{1,0:T(8,128)(2,1)S(1)}, bf16[128,256]{1,0:T(8,128)(2,1)}, u32[]{:S(2)}) copy-start(bf16[128,256]{1,0:T(8,128)(2,1)} %constant.23.clone.last) | copy-start | bytes 196612
  3.8 56.7 %copy-start.7 = (f32[64,128]{1,0:T(8,128)S(1)}, f32[64,128]{1,0:T(8,128)}, u32[]{:S(2)}) copy-start(f32[64,128]{1,0:T(8,128)} %constant.19.clone.twist_masked) | copy-start | bytes 98308
  3.8 56.7 %copy-start.8 = (f32[64,128]{1,0:T(8,128)S(1)}, f32[64,128]{1,0:T(8,128)}, u32[]{:S(2)}) copy-start(f32[64,128]{1,0:T(8,128)} %constant.18.clone.twist_imag) | copy-start | bytes 98308
  3.8 56.7 %copy-start.9 = (f32[64,128]{1,0:T(8,128)S(1)}, f32[64,128]{1,0:T(8,128)}, u32[]{:S(2)}) copy-start(f32[64,128]{1,0:T(8,128)} %constant.17.clone.twist_real) | copy-start | bytes 98308
  3.9 56.7 %copy-start.10 = (bf16[128,128]{1,0:T(8,128)(2,1)S(1)}, bf16[128,128]{1,0:T(8,128)(2,1)}, u32[]{:S(2)}) copy-start(bf16[128,128]{1,0:T(8,128)(2,1)} %constant.16.clone.first) | copy-start | bytes 98308
  3.9 56.7 %copy-start.11 = (f32[2,128]{1,0:T(2,128)S(1)}, f32[2,128]{1,0:T(2,128)}, u32[]{:S(2)}) copy-start(f32[2,128]{1,0:T(2,128)} %constant.20.clone.middle_twist) | copy-start | bytes 3076
  69.1 49.0 %copy-start = (bf16[256,1024]{1,0:T(8,128)(2,1)S(1)}, bf16[256,1024]{1,0:T(8,128)(2,1)}, u32[]{:S(2)}) copy-start(bf16[256,1024]{1,0:T(8,128)(2,1)} %query.3) | copy-start | bytes 1572868
  69.1 49.0 %copy-start.1 = (bf16[256,1024]{1,0:T(8,128)(2,1)S(1)}, bf16[256,1024]{1,0:T(8,128)(2,1)}, u32[]{:S(2)}) copy-start(bf16[256,1024]{1,0:T(8,128)(2,1)} %key.3) | copy-start | bytes 1572868
  69.1 49.0 %copy-start.2 = (bf16[256,1024]{1,0:T(8,128)(2,1)S(1)}, bf16[256,1024]{1,0:T(8,128)(2,1)}, u32[]{:S(2)}) copy-start(bf16[256,1024]{1,0:T(8,128)(2,1)} %value.3) | copy-start | bytes 1572868
  69.1 49.0 %copy-start.3 = (bf16[256,1024]{1,0:T(8,128)(2,1)S(1)}, bf16[256,1024]{1,0:T(8,128)(2,1)}, u32[]{:S(2)}) copy-start(bf16[256,1024]{1,0:T(8,128)(2,1)} %cotangent.3) | copy-start | bytes 1572868

commit v8 on v7

--- a/solution.py
+++ b/solution.py
@@ -424,7 +424,7 @@
 
 def scatter(query, key, value, cotangent, back, taps_shape):
     positions, width = query.shape
-    pieces = PIECES
+    pieces = 2 * PIECES
     anywhere = pl.BlockSpec(memory_space=pl.ANY)
     return pl.pallas_call(
         scatter_kernel,

time: 122 us -> 122 us (level)
  no operation moved by 1% of the time
where the time goes in v8:
time: 122 us; the launch traced here: 120 us
  blocking collectives  106 us (87%)
  Pallas kernels  13.6 us (11%)
    all_to_all x1, blocking collectives, local(): lax.all_to_all(sent, everyone, split_axis=0, concat_axis=0, tiled=True)  56.6 us
    all_to_all x1, blocking collectives, local(): lax.all_to_all(made, everyone, split_axis=0, concat_axis=0, tiled=True)  49 us
    pallas_call x1, Pallas kernels, long_convolution(): pl.pallas_call(long_kernel, out_shape=jax.ShapeDtypeStruct(received.shape...  8.51 us
    pallas_call x1, Pallas kernels, gather(): pl.pallas_call(gather_kernel, in_specs=[anywhere] * 5, out_specs=anywhere...  3.15 us

profile of v8, /device:TPU:34, one launch (start us, length us, event | category | flops | bytes accessed | tf_op | source)
XLA Modules:
  0.0 120.1 jit_solution(7201096180191725902)
XLA Ops:
  0.6 3.1 %shard_map.164 = bf16[6144,128]{1,0:T(8,128)(2,1)} custom-call(bf16[256,1024]{1,0:T(8,128)(2,1)} %query.3, bf16[256,1024]{1,0:T(8,128)(2,1)} %key.3, bf16[256,1024]{1,0:T(8,128)(2,1)} %value.3, bf16[256,1024]{1,0:T(8,128)(2,1)} %cotangent.3, bf16[32,8192]{1,0:T(8,128)(2,1)} %taps.1), custom_call_target="tpu_custom_call" | custom-call | flops 1000000 | bytes 4194304 | tf_op jit(solution)/shard_map/pallas_call | solution.py:407
  3.8 0.0 copy-start.4
  3.8 0.0 copy-start.5
  3.8 0.0 copy-start.6
  3.8 0.0 copy-start.7
  3.8 0.0 copy-start.8
  3.8 0.0 copy-start.9
  3.9 0.0 copy-start.10
  3.9 0.0 copy-start.11
  3.9 56.6 %all_to_all.22 = bf16[256,24,128]{2,1,0:T(8,128)(2,1)S(1)} all-to-all(bf16[256,24,128]{2,1,0:T(8,128)(2,1)} %bitcast.7), channel_id=1, replica_groups=mesh['ctx'=32,'tp'=8] {'ctx','tp'}, dimensions={0} | all-to-all | bytes 3145728 | tf_op jit(solution)/shard_map/all_to_all | solution.py:471
  60.5 0.0 copy-done.4
  60.5 0.0 copy-done.5
  60.5 0.0 copy-done.6
  60.5 0.0 copy-done.7
  60.5 0.0 copy-done.8
  60.5 0.0 copy-done.9
  60.5 0.0 copy-done.10
  60.6 0.0 copy-done.11
  60.6 8.5 %shard_map.165 = bf16[6144,128]{1,0:T(8,128)(2,1)S(1)} custom-call(bf16[6144,128]{1,0:T(8,128)(2,1)S(1)} %bitcast.5, bf16[128,128]{1,0:T(8,128)(2,1)S(1)} %copy-done.10, f32[64,128]{1,0:T(8,128)S(1)} %copy-done.9, f32[64,128]{1,0:T(8,128)S(1)} %copy-done.8, f32[64,128]{1,0:T(8,128)S(1)} %copy-done.7, f32[2,128]{1,0:T(2,128)S(1)} %copy-done.11, ...), custom_call_target="tpu_custom_call" | custom-call | flops 10000000000 | bytes 3145728 | tf_op jit(solution)/shard_map/pallas_call | solution.py:451
  69.1 0.0 copy-start
  69.1 0.0 copy-start.1
  69.1 0.0 copy-start.2
  69.1 0.0 copy-start.3
  69.1 49.0 %all_to_all.23 = bf16[256,24,128]{2,1,0:T(8,128)(2,1)S(1)} all-to-all(bf16[256,24,128]{2,1,0:T(8,128)(2,1)S(1)} %bitcast.6), channel_id=1, replica_groups=mesh['ctx'=32,'tp'=8] {'ctx','tp'}, dimensions={0} | all-to-all | bytes 3145728 | tf_op jit(solution)/shard_map/all_to_all | solution.py:473
  118.1 0.0 copy-done
  118.1 0.0 copy-done.1
  118.1 0.0 copy-done.2
  118.1 0.0 copy-done.3
  118.2 1.9 %shard_map.166 = (bf16[256,1024]{1,0:T(8,128)(2,1)}, bf16[256,1024]{1,0:T(8,128)(2,1)}, bf16[256,1024]{1,0:T(8,128)(2,1)}, bf16[256,1024]{1,0:T(8,128)(2,1)}, bf16[32,8192]{1,0:T(8,128)(2,1)}) custom-call(bf16[256,1024]{1,0:T(8,128)(2,1)S(1)} %copy-done, bf16[256,1024]{1,0:T(8,128)(2,1)S(1)} %copy-done.1, bf16[256,1024]{1,0:T(8,128)(2,1)S(1)} %copy-done.2, ...), custom_call_target="tpu_custom_call" | custom-call | flops 1000000 | bytes 6291456 | tf_op jit(solution)/shard_map/pallas_call | solution.py:429
Async XLA Ops:
  3.8 56.7 %copy-start.4 = (bf16[768,256]{1,0:T(8,128)(2,1)S(1)}, bf16[768,256]{1,0:T(8,128)(2,1)}, u32[]{:S(2)}) copy-start(bf16[768,256]{1,0:T(8,128)(2,1)} %constant.22.clone.back) | copy-start | bytes 1179652
  3.8 56.7 %copy-start.5 = (bf16[768,256]{1,0:T(8,128)(2,1)S(1)}, bf16[768,256]{1,0:T(8,128)(2,1)}, u32[]{:S(2)}) copy-start(bf16[768,256]{1,0:T(8,128)(2,1)} %constant.21.clone.ahead) | copy-start | bytes 1179652
  3.8 56.7 %copy-start.6 = (bf16[128,256]{1,0:T(8,128)(2,1)S(1)}, bf16[128,256]{1,0:T(8,128)(2,1)}, u32[]{:S(2)}) copy-start(bf16[128,256]{1,0:T(8,128)(2,1)} %constant.23.clone.last) | copy-start | bytes 196612
  3.8 56.7 %copy-start.7 = (f32[64,128]{1,0:T(8,128)S(1)}, f32[64,128]{1,0:T(8,128)}, u32[]{:S(2)}) copy-start(f32[64,128]{1,0:T(8,128)} %constant.19.clone.twist_masked) | copy-start | bytes 98308
  3.8 56.7 %copy-start.8 = (f32[64,128]{1,0:T(8,128)S(1)}, f32[64,128]{1,0:T(8,128)}, u32[]{:S(2)}) copy-start(f32[64,128]{1,0:T(8,128)} %constant.18.clone.twist_imag) | copy-start | bytes 98308
  3.8 56.7 %copy-start.9 = (f32[64,128]{1,0:T(8,128)S(1)}, f32[64,128]{1,0:T(8,128)}, u32[]{:S(2)}) copy-start(f32[64,128]{1,0:T(8,128)} %constant.17.clone.twist_real) | copy-start | bytes 98308
  3.9 56.7 %copy-start.10 = (bf16[128,128]{1,0:T(8,128)(2,1)S(1)}, bf16[128,128]{1,0:T(8,128)(2,1)}, u32[]{:S(2)}) copy-start(bf16[128,128]{1,0:T(8,128)(2,1)} %constant.16.clone.first) | copy-start | bytes 98308
  3.9 56.7 %copy-start.11 = (f32[2,128]{1,0:T(2,128)S(1)}, f32[2,128]{1,0:T(2,128)}, u32[]{:S(2)}) copy-start(f32[2,128]{1,0:T(2,128)} %constant.20.clone.middle_twist) | copy-start | bytes 3076
  69.1 49.0 %copy-start = (bf16[256,1024]{1,0:T(8,128)(2,1)S(1)}, bf16[256,1024]{1,0:T(8,128)(2,1)}, u32[]{:S(2)}) copy-start(bf16[256,1024]{1,0:T(8,128)(2,1)} %query.3) | copy-start | bytes 1572868
  69.1 49.0 %copy-start.1 = (bf16[256,1024]{1,0:T(8,128)(2,1)S(1)}, bf16[256,1024]{1,0:T(8,128)(2,1)}, u32[]{:S(2)}) copy-start(bf16[256,1024]{1,0:T(8,128)(2,1)} %key.3) | copy-start | bytes 1572868
  69.1 49.0 %copy-start.2 = (bf16[256,1024]{1,0:T(8,128)(2,1)S(1)}, bf16[256,1024]{1,0:T(8,128)(2,1)}, u32[]{:S(2)}) copy-start(bf16[256,1024]{1,0:T(8,128)(2,1)} %value.3) | copy-start | bytes 1572868
  69.1 49.0 %copy-start.3 = (bf16[256,1024]{1,0:T(8,128)(2,1)S(1)}, bf16[256,1024]{1,0:T(8,128)(2,1)}, u32[]{:S(2)}) copy-start(bf16[256,1024]{1,0:T(8,128)(2,1)} %cotangent.3) | copy-start | bytes 1572868
